TPU v7x, 256 devices: a whole 4x4x8 slice. The times are simulated.
256 devices in a mesh: rep: 4 (over x_lo, core), cls: 64 (over x_hi, y, z).
Axes of the slice: x: 4 (x_hi: 2, x_lo: 2; x = x_hi * 2 + x_lo), y: 4, z: 8, core: 2. Of those that a mesh axis runs over, the one named last changes fastest.
Arguments:
- features: bfloat16 [8192, 512], P(('rep', 'cls')), may hold values from -6 to 6
- centers: bfloat16 [131072, 512], P('cls'), may hold values from -0.25 to 0.25
- momentum: float32 [131072, 512], P('cls'), may hold values from -6 to 6
- sample_rows: int32 [98304], P('cls'), may hold values from 0 to 2047, as said below
- labels: int32 [8192], P(('rep', 'cls')), may hold values from 0 to 131071, as said below
Outputs:
- feature_grad: float32 [8192, 512], P(('rep', 'cls'))
- sample_loss: float32 [8192], P(('rep', 'cls'))
- new_centers: bfloat16 [98304, 512], P('cls')
- new_momentum: float32 [98304, 512], P('cls')
Inputs may be any that keep to these rules, and one draw needn't show every extreme that they name: `sample_rows`: within each class shard's block of 1536 entries the rows are distinct, and 0 and 2047 are among them. `labels`: each label is k * 2048 + r for a shard k and a row r in shard k's block of sample_rows.
All inputs are finite; a program needn't handle non-finite values.
Results may differ from a plain program's by a relative error of at most 0.011.
Values may be sent and summed in bfloat16 or wider, within the bound.
A program may use at most 128 MiB of HBM per device.

v0:
```python
import jax
import jax.numpy as jnp
from jax import lax
from jax.sharding import PartitionSpec as P

eps = 1e-06
logit_scale = 64.0
margin = 0.35
moment_rate = 0.9
learn_rate = 0.1


def normalise(values):
    floats = values.astype(jnp.float32)
    norm = jnp.sqrt(jnp.sum(floats * floats, axis=-1, keepdims=True) + eps)
    return (floats / norm, norm)


def apply_update(grad, rows_w, rows_m):
    unit, norm = normalise(rows_w)
    step_dir = (grad - unit * jnp.sum(unit * grad, axis=1, keepdims=True)) / norm
    new_m = moment_rate * rows_m + step_dir
    new_w = (rows_w.astype(jnp.float32) - learn_rate * new_m).astype(jnp.bfloat16)
    return (new_w, new_m)


def local(features, centers, momentum, sample_rows, labels):
    local_rows = features.shape[0]
    unit_feat, feat_norm = normalise(features)
    feat_bf = unit_feat.astype(jnp.bfloat16)
    center_rows = jnp.take(centers, sample_rows, axis=0)
    moment_rows = jnp.take(momentum, sample_rows, axis=0)
    unit_cent, cent_norm = normalise(center_rows)
    cent_bf = unit_cent.astype(jnp.bfloat16)
    class_ids = sample_rows + lax.axis_index("cls") * centers.shape[0]
    gathered, group_labels = (
        lax.all_gather(feat_bf, "cls", axis=0, tiled=True),
        lax.all_gather(labels, "cls", axis=0, tiled=True),
    )
    matches = (group_labels[:, None] == class_ids[None, :]).astype(jnp.float32)
    cosine = lax.dot_general(
        gathered, cent_bf, (((1,), (1,)), ((), ())), preferred_element_type=jnp.float32
    )
    logits = logit_scale * (cosine - margin * matches)
    expo = jnp.exp(logits - logit_scale)
    totals, positive = lax.psum((jnp.sum(expo, axis=1), jnp.sum(matches * logits, axis=1)), "cls")
    own_first = lax.axis_index("cls") * local_rows
    own_totals = lax.dynamic_slice_in_dim(totals, own_first, local_rows)
    own_positive = lax.dynamic_slice_in_dim(positive, own_first, local_rows)
    sample_loss = jnp.log(own_totals) + logit_scale - own_positive
    soft = (expo / totals[:, None] - matches).astype(jnp.bfloat16)
    grad_unit = lax.psum_scatter(
        logit_scale * jnp.dot(soft, cent_bf, preferred_element_type=jnp.float32),
        "cls",
        scatter_dimension=0,
        tiled=True,
    )
    feature_grad = (
        grad_unit - unit_feat * jnp.sum(unit_feat * grad_unit, axis=1, keepdims=True)
    ) / feat_norm
    grad_local = logit_scale * lax.dot_general(
        soft, gathered, (((0,), (0,)), ((), ())), preferred_element_type=jnp.float32
    )
    grad_cent = lax.psum(grad_local.astype(jnp.bfloat16), "rep").astype(jnp.float32)
    new_centers, new_momentum = apply_update(grad_cent, center_rows, moment_rows)
    return (feature_grad, sample_loss, new_centers, new_momentum)


def solution(mesh):
    in_specs = (
        P(("rep", "cls"), None),
        P("cls", None),
        P("cls", None),
        P("cls"),
        P(("rep", "cls")),
    )
    out_specs = (P(("rep", "cls"), None), P(("rep", "cls")), P("cls", None), P("cls", None))
    return jax.shard_map(local, mesh=mesh, in_specs=in_specs, out_specs=out_specs, check_vma=False)
```

profile of v0, /device:TPU:2, one launch (start us, length us, event | category | flops | bytes accessed | tf_op | source)
XLA Modules:
  0.0 942.4 jit_solution(12370017277090574833)
XLA Ops:
  7.2 0.0 copy-start
  7.2 0.0 all-gather.2.cloned.1.call-start
  7.2 1.0 fusion.14
  8.2 1.5 fusion.15
  9.7 0.0 all-gather.2.cloned.1.call-update
  9.7 0.0 all-reduce.4.cloned.1.call-start
  9.8 0.7 compare_select_fusion.2
  10.5 0.0 copy-done
  10.5 0.0 copy-start.8
  10.5 0.0 copy-start.7
  10.5 0.0 copy-start.5
  10.6 5.4 gather_fusion
  16.0 0.0 copy-done.8
  16.0 0.6 dynamic-slice
  17.2 0.0 copy-done.7
  17.2 0.3 dynamic-update-slice
  17.5 27.8 %all-reduce = s32[2048]{0:T(1024)S(1)} all-reduce(s32[2048]{0:T(1024)S(1)} %dynamic-update-slice), channel_id=1, replica_groups=mesh['rep'=4,'cls'=64] {'cls'}, use_global_device_ids=true, to_apply=%add | all-reduce | flops 2048 | bytes 16384
  45.3 0.0 copy-done.5
  45.4 2.1 fusion.9
  47.4 85.4 %all-gather.2.cloned.1.call-done = bf16[2048,512]{1,0:T(8,128)(2,1)} async-done(((bf16[32,512]{1,0:T(8,128)(2,1)}), bf16[2048,512]{1,0:T(8,128)(2,1)}) %all-gather.2.cloned.1.call-update) | async-done | bytes 2097168 | tf_op jit(solution)/shard_map/all_gather | solution.py:37
  132.8 10.2 %fusion.4 = (f32[2048]{0:T(1024)S(1)}, f32[2048]{0:T(1024)S(1)}, f32[2048,1536]{0,1:T(8,128)}) fusion(s32[2048]{0:T(1024)S(1)} %all-reduce, s32[1536]{0:T(1024)S(1)} %get-tuple-element.11, bf16[2048,512]{1,0:T(8,128)(2,1)} %all-gather.2.cloned.1.call-done, f32[1536]{0:T(1024)S(1)} %add_sqrt_fusion, bf16[1536,512]{1,0:T(8,128)(2,1)} %gather_fusion, ...), kind=kOutput, calls=%fused_computation.9 | convolution fusion | flops 3249532928 | bytes 16291328 | tf_op jit(solution)/shard_map/dot_general | solution.py:41
  143.1 355.5 %all-reduce.1 = (f32[2048]{0:T(1024)S(1)}, f32[2048]{0:T(1024)S(1)}) all-reduce(f32[2048]{0:T(1024)S(1)} %get-tuple-element.5, f32[2048]{0:T(1024)S(1)} %get-tuple-element.4), channel_id=1, replica_groups=mesh['rep'=4,'cls'=64] {'cls'}, use_global_device_ids=true, to_apply=%region_3.4 | all-reduce | flops 4096 | bytes 32768 | tf_op jit(solution)/shard_map/psum | solution.py:46
  498.6 0.0 copy-start.6
  498.6 7.0 fusion.3
  505.6 0.0 copy-start.2
  505.6 2.7 copy-done.2
  508.3 0.0 copy-done.6
  508.3 4.5 fusion.11
  512.8 0.0 all-reduce.4.cloned.1.call-update
  512.9 0.2 reduce-scatter.2.cloned.1.call-start
  513.1 8.8 convolution_multiply_fusion.1
  521.9 0.0 reduce-scatter.2.cloned.1.call-update
  522.0 7.9 gather_fusion.1
  529.8 0.6 dynamic-slice_subtract_fusion
  530.4 29.3 %all-reduce.4.cloned.1.call-done = bf16[1536,512]{1,0:T(8,128)(2,1)} async-done(((bf16[1536,512]{1,0:T(8,128)(2,1)}), bf16[1536,512]{1,0:T(8,128)(2,1)}) %all-reduce.4.cloned.1.call-update) | async-done | bytes 1572880 | tf_op jit(solution)/shard_map/psum | solution.py:64
  559.7 0.0 copy-start.1
  559.7 0.0 copy-start.3
  559.7 3.0 fusion.6
  562.7 0.0 copy-done.1
  562.8 0.0 copy-done.3
  562.8 0.0 copy-start.4
  562.8 4.6 fusion.10
  567.4 365.9 %reduce-scatter.2.cloned.1.call-done = f32[32,512]{1,0:T(8,128)} async-done(((f32[2048,512]{1,0:T(8,128)}), f32[32,512]{1,0:T(8,128)}) %reduce-scatter.2.cloned.1.call-update) | async-done | bytes 65552 | tf_op jit(solution)/shard_map/reduce_scatter | solution.py:52
  933.3 0.0 copy-done.4
  933.3 1.0 multiply_reduce_fusion
  934.3 1.6 subtract_divide_fusion
  (5 shorter events, 0.0 us)
Async XLA Ops:
  7.2 3.3 copy-start
  7.2 125.6 %all-gather.2.cloned.1.call-start = ((), (), s32[]{:S(2)}) async-start(), calls=%async_computation.1 | async-start | bytes 2129920 | tf_op jit(solution)/shard_map/all_gather | solution.py:37
  9.7 550.0 %all-reduce.4.cloned.1.call-start = ((), (), s32[]{:S(2)}) async-start(), calls=%async_computation.3 | async-start | bytes 3145728 | tf_op jit(solution)/shard_map/psum | solution.py:64
  10.5 5.4 copy-start.8
  10.5 6.7 copy-start.7
  10.5 34.8 %copy-start.5 = (s32[1536]{0:T(1024)S(1)}, s32[1536]{0:T(1024)}, u32[]{:S(2)}) copy-start(s32[1536]{0:T(1024)} %param.8) | copy-start | bytes 18436
  498.6 9.7 %copy-start.6 = (bf16[2048,512]{1,0:T(8,128)(2,1)S(1)}, bf16[2048,512]{1,0:T(8,128)(2,1)}, u32[]{:S(2)}) copy-start(bf16[2048,512]{1,0:T(8,128)(2,1)} %all-gather.2.cloned.1.call-done) | copy-start | bytes 6291460
  505.6 2.7 copy-start.2
  512.9 420.4 %reduce-scatter.2.cloned.1.call-start = ((), (), s32[]{:S(2)}) async-start(), calls=%async_computation.2 | async-start | bytes 4259840 | tf_op jit(solution)/shard_map/reduce_scatter | solution.py:52
  559.7 3.0 copy-start.1
  559.7 3.1 copy-start.3
  562.8 370.5 %copy-start.4 = (bf16[32,512]{1,0:T(8,128)(2,1)S(1)}, bf16[32,512]{1,0:T(8,128)(2,1)}, u32[]{:S(2)}) copy-start(bf16[32,512]{1,0:T(8,128)(2,1)} %param.5) | copy-start | bytes 98308
Sparse Core Ops, SparseCore 0:
  12.1 120.6 all-gather.1
  513.0 46.6 all-reduce.3
  562.2 371.0 reduce-scatter.1
where the time goes:
time: 943 us; the launch traced here: 942 us
  waiting for transfers between devices  481 us (51%)
  blocking collectives  383 us (41%)
  matrix products  23.6 us (3%)
  other arithmetic  23.2 us (2%)
  local copies, waits for them, and re-layouts  16.9 us (2%)
  between operations  14.5 us (2%)
    reduce_scatter x1, waiting for transfers between devices, local(): lax.psum_scatter(logit_scale * jnp.dot(soft, cent_bf, preferred_element_t...  366 us
    psum x1, blocking collectives, local(): lax.psum((jnp.sum(expo, axis=1), jnp.sum(matches * logits, axis=1)), 'cls')  356 us
    all_gather x1, waiting for transfers between devices, local(): lax.all_gather(feat_bf, 'cls', axis=0, tiled=True)  85.4 us
    psum x1, waiting for transfers between devices, local(): lax.psum(grad_local.astype(jnp.bfloat16), 'rep').astype(jnp.float32)  29.3 us
    unnamed x1, blocking collectives  27.8 us
  transfers between devices with their start and end apart: 3, of which 3 were waited for; matrix products, arithmetic and copies ran while one was open for 4% of the time, Pallas kernels for 0%

commit v1 on v0

v1 whole, which is shorter than its diff:
```python
import math

import jax
import jax.numpy as jnp
from jax import lax
from jax.experimental import pallas as pl
from jax.experimental.pallas import tpu as pltpu
from jax.sharding import PartitionSpec as P

MESH = pl.DeviceIdType.MESH

EPS = 1e-06
SCALE = 64.0
MARGIN = 0.35
MOMENT_RATE = 0.9
LEARN_RATE = 0.1

NX, NY, NZ = 2, 4, 8
TOK = 32
HALF = TOK // 2
GROUP = TOK * NX * NY * NZ
D = 512
SLOTS = 1536
ROWS = 2048
SB = 256
NSB = SLOTS // SB
OWN = SLOTS // 2
NCB = OWN // SB
LANES = 128
LOG2E = math.log2(math.e)
F32, BF16 = jnp.float32, jnp.bfloat16


class Sems:
    def __init__(self):
        self.n = 0

    def take(self, count):
        first = self.n
        self.n += count
        return first


_s = Sems()
AG1A, AG1B = _s.take(7), _s.take(15)
AGAP, AGAM, AGBP, AGBM = _s.take(4), _s.take(3), _s.take(2), _s.take(1)
LAB1, LAB2, TOT1, TOT2 = _s.take(7), _s.take(7), _s.take(7), _s.take(7)
CORE1, XLO, CORE2 = _s.take(3), _s.take(3), _s.take(3)
RSAP, RSAM, RSBP, RSBM = _s.take(4), _s.take(3), _s.take(2), _s.take(1)
RS2A, RS2B = _s.take(7), _s.take(15)
N_SEMS = _s.n


def wrap(value, n):
    return lax.rem(value + n, n)


def rows16(start, count):
    return pl.ds(pl.multiple_of(start, 16), count)


def lanes(start, count):
    return pl.ds(pl.multiple_of(start, LANES), count)


def row_norm(floats):
    return jnp.sqrt(jnp.sum(floats * floats, axis=-1, keepdims=True) + EPS)


def kernel(
    feat_ref, ids_ref, lab_ref, rows_ref, cent_hbm, mom_hbm,
    fgrad_ref, loss_ref, newc_ref, newm_ref,
    cent_v, mom_v, feats, crow, cbf, cbt, momg, expo, soft, ut,
    labs, lab1, lab1s, lab2, tot, tot1, tot1s, tot2, rtot,
    csend, cown, crecv, xsend, xrecv, gsum,
    sap, rap, sam, ram, sbp, rbp, sbm, rbm,
    wa, wb, wab, wbb, r2a, r2b,
    ssem, rsem, lsem,
):
    rep, cls = lax.axis_index("rep"), lax.axis_index("cls")
    x, y, z = lax.div(cls, NY * NZ), lax.rem(lax.div(cls, NZ), NY), lax.rem(cls, NZ)
    x_lo, core = lax.div(rep, 2), lax.rem(rep, 2)

    def at(x, y, z):
        return (rep, (x * NY + y) * NZ + z)

    xy = [(k % NX, k // NX) for k in range(1, NX * NY)]
    xz = [(k % NX, k // NX) for k in range(1, NX * NZ)]

    def flip(dx):
        return x if dx == 0 else 1 - x

    def xy_to(dx, dy):
        return flip(dx), wrap(y + dy, NY)

    def xy_from(dx, dy):
        return flip(dx), wrap(y - dy, NY)

    def xz_to(dx, dz):
        return flip(dx), wrap(z + dz, NZ)

    def xz_from(dx, dz):
        return flip(dx), wrap(z - dz, NZ)

    core_peer = (x_lo * 2 + 1 - core, cls)
    xlo_peer = ((1 - x_lo) * 2 + core, cls)
    up_z, down_z = at(x, y, wrap(z + 1, NZ)), at(x, y, wrap(z - 1, NZ))
    up_y, down_y = at(x, wrap(y + 1, NY), z), at(x, wrap(y - 1, NY), z)

    pending = []

    def push(src, dst, sem, device):
        copy = pltpu.make_async_remote_copy(
            src_ref=src, dst_ref=dst, send_sem=ssem.at[sem], recv_sem=rsem.at[sem],
            device_id=device, device_id_type=MESH,
        )
        copy.start()
        pending.append(copy)

    def arrived(dst, sem):
        pltpu.make_async_remote_copy(
            src_ref=dst, dst_ref=dst, send_sem=ssem.at[sem], recv_sem=rsem.at[sem],
            device_id=core_peer, device_id_type=MESH,
        ).wait_recv()

    load_c = pltpu.make_async_copy(cent_hbm, cent_v, lsem.at[0])
    load_m = pltpu.make_async_copy(mom_hbm, mom_v, lsem.at[1])
    load_c.start()
    load_m.start()

    barrier = pltpu.get_barrier_semaphore()
    greet = [at(*xy_to(dx, dy), z) for dx, dy in xy]
    greet += [at(xz_to(dx, dz)[0], y, xz_to(dx, dz)[1]) for dx, dz in xz if dz != 0]
    greet += [core_peer, xlo_peer]
    for device in greet:
        pl.semaphore_signal(barrier, inc=1, device_id=device, device_id_type=MESH)

    def row_a(x, y, z):
        return z * 128 + (x * NY + y) * HALF

    def row_b(x, y, z):
        return GROUP // 2 + y * 256 + (x * NZ + z) * HALF

    floats = feat_ref[...].astype(F32)
    unit = (floats / row_norm(floats)).astype(BF16)
    own_a, own_b = rows16(row_a(x, y, z), HALF), rows16(row_b(x, y, z), HALF)
    feats[own_a, :] = unit[:HALF]
    feats[own_b, :] = unit[HALF:]

    pl.semaphore_wait(barrier, len(greet))

    for k, off in enumerate(xy):
        px, py = xy_to(*off)
        push(feats.at[own_a, :], feats.at[own_a, :], AG1A + k, at(px, py, z))
    for k, off in enumerate(xy):
        px, py = xy_to(*off)
        push(lab_ref, lab1.at[k], LAB1 + k, at(px, py, z))
    for k, off in enumerate(xz):
        px, pz = xz_to(*off)
        push(feats.at[own_b, :], feats.at[own_b, :], AG1B + k, at(px, y, pz))

    load_c.wait()

    def pick(sb, carry):
        part = pl.ds(pl.multiple_of(sb * SB, SB), SB)
        ids = ids_ref[part, :] - cls * ROWS
        col = lax.broadcasted_iota(jnp.int32, (SB, LANES), 1)
        hot = jnp.concatenate(
            [jnp.where(ids == col + j * LANES, 1.0, 0.0).astype(BF16) for j in range(ROWS // LANES)],
            axis=1,
        )
        got = jnp.dot(hot, cent_v[...], preferred_element_type=F32)
        crow[part, :] = got.astype(BF16)
        cbf[part, :] = (got / row_norm(got)).astype(BF16)
        return carry

    lax.fori_loop(0, NSB, pick, 0)

    for k, off in enumerate(xy):
        px, py = xy_from(*off)
        arrived(feats.at[rows16(row_a(px, py, z), HALF), :], AG1A + k)

    def blk_a(zb):
        return feats.at[rows16(zb * 128, 128), :]

    def blk_b(yb):
        return feats.at[rows16(GROUP // 2 + yb * 256, 256), :]

    push(blk_a(z), blk_a(z), AGAP, up_z)
    push(blk_a(z), blk_a(z), AGAM, down_z)
    for k, off in enumerate(xz):
        px, pz = xz_from(*off)
        arrived(feats.at[rows16(row_b(px, y, pz), HALF), :], AG1B + k)
    push(blk_b(y), blk_b(y), AGBP, up_y)
    push(blk_b(y), blk_b(y), AGBM, down_y)

    for k in range(7):
        arrived(lab1.at[k], LAB1 + k)
    lab1s[...] = lab_ref[...] + sum(lab1[k] for k in range(7))
    for k in range(7):
        push(lab1s, lab2.at[k], LAB2 + k, at(x, y, wrap(z + k + 1, NZ)))
    for k in range(7):
        arrived(lab2.at[k], LAB2 + k)
    labs[...] = lab1s[...] + sum(lab2[k] for k in range(7))

    def logits(start, nb, lrow):
        n = nb // LANES
        block = feats[rows16(start, nb), :]
        rows = [labs[pl.ds(lrow + h, 1), :] for h in range(n)]

        def body(sb, carry):
            part = pl.ds(pl.multiple_of(sb * SB, SB), SB)
            cosine = lax.dot_general(
                cbf[part, :], block, (((1,), (1,)), ((), ())), preferred_element_type=F32
            )
            ids = ids_ref[part, :]
            out = []
            for h in range(n):
                cos_h = cosine[:, h * LANES : (h + 1) * LANES]
                match = ids == rows[h]
                logit = SCALE * (cos_h - jnp.where(match, MARGIN, 0.0))
                e = jnp.exp2((logit - SCALE) * LOG2E)
                expo[part, lanes(start + h * LANES, LANES)] = e
                out.append(carry[2 * h] + jnp.sum(e.reshape(SB // 8, 8, LANES), axis=0))
                hit = jnp.where(match, logit, 0.0)
                out.append(carry[2 * h + 1] + jnp.sum(hit.reshape(SB // 8, 8, LANES), axis=0))
            return tuple(out)

        zero = jnp.zeros((8, LANES), F32)
        sums = lax.fori_loop(0, NSB, body, (zero,) * (2 * n))
        for h in range(n):
            tot[pl.ds(lrow + h, 1), :] = jnp.sum(sums[2 * h], axis=0, keepdims=True)
            tot[pl.ds(16 + lrow + h, 1), :] = jnp.sum(sums[2 * h + 1], axis=0, keepdims=True)

    def logits_a(zb):
        logits(zb * 128, 128, zb)

    def logits_b(yb):
        logits(GROUP // 2 + yb * 256, 256, 8 + yb * 2)

    logits_a(z)
    logits_b(y)
    for s in range(4):
        zp, zm = wrap(z - 1 - s, NZ), wrap(z + 1 + s, NZ)
        arrived(blk_a(zp), AGAP + s)
        if s < 3:
            push(blk_a(zp), blk_a(zp), AGAP + s + 1, up_z)
            arrived(blk_a(zm), AGAM + s)
        if s < 2:
            push(blk_a(zm), blk_a(zm), AGAM + s + 1, down_z)
        if s == 1:
            yp, ym = wrap(y - 1, NY), wrap(y + 1, NY)
            arrived(blk_b(yp), AGBP)
            push(blk_b(yp), blk_b(yp), AGBP + 1, up_y)
        logits_a(zp)
        if s < 3:
            logits_a(zm)
        if s == 1:
            arrived(blk_b(ym), AGBM)
            logits_b(yp)
            logits_b(ym)
    y2 = wrap(y - 2, NY)
    arrived(blk_b(y2), AGBP + 1)
    logits_b(y2)

    for k, off in enumerate(xy):
        px, py = xy_to(*off)
        push(tot, tot1.at[k], TOT1 + k, at(px, py, z))

    load_m.wait()

    def pick_m(j, carry):
        for u in range(16):
            i = j * 16 + u
            momg[pl.ds(i, 1), :] = mom_v[pl.ds(rows_ref[i], 1), :]
        return carry

    lax.fori_loop(0, SLOTS // 32, pick_m, 0)
    for k in range(7):
        arrived(tot1.at[k], TOT1 + k)
    tot1s[...] = tot[...] + sum(tot1[k] for k in range(7))
    for k in range(7):
        push(tot1s, tot2.at[k], TOT2 + k, at(x, y, wrap(z + k + 1, NZ)))

    lax.fori_loop(SLOTS // 32, SLOTS // 16, pick_m, 0)
    for sb in range(NSB):
        cbt[:, sb * SB : (sb + 1) * SB] = cbf[sb * SB : (sb + 1) * SB, :].T

    for k in range(7):
        arrived(tot2.at[k], TOT2 + k)
    whole = tot1s[...] + sum(tot2[k] for k in range(7))
    totals, positive = whole[:16], whole[16:]
    rtot[...] = 1.0 / totals
    loss_ref[...] = jnp.log(totals) + SCALE - positive

    def center_grad(first):
        part = pl.ds(pl.multiple_of(first, SB), SB)
        ids = ids_ref[part, :]

        def body(k, carry):
            col = lanes(k * LANES, LANES)
            match = ids == labs[pl.ds(k, 1), :]
            value = expo[part, col] * rtot[pl.ds(k, 1), :]
            soft[part, col] = (value - jnp.where(match, 1.0, 0.0)).astype(BF16)
            return carry

        lax.fori_loop(0, GROUP // LANES, body, 0)
        return SCALE * jnp.dot(soft[part, :], feats[...], preferred_element_type=F32)

    mine, other = core * OWN, (1 - core) * OWN

    def join_cores(i):
        arrived(crecv.at[i], CORE1 + i)
        xsend[i] = (cown[i].astype(F32) + crecv[i].astype(F32)).astype(BF16)
        push(xsend.at[i], xrecv.at[i], XLO + i, xlo_peer)

    for i in range(NCB):
        csend[i] = center_grad(other + i * SB).astype(BF16)
        push(csend.at[i], crecv.at[i], CORE1 + i, core_peer)
        cown[i] = center_grad(mine + i * SB).astype(BF16)
        if i:
            join_cores(i - 1)
    join_cores(NCB - 1)

    def feature_part(k, carry):
        col = lanes(k * 256, 256)
        ut[:, col] = SCALE * jnp.dot(cbt[...], soft[:, col], preferred_element_type=F32)
        return carry

    lax.fori_loop(0, GROUP // 256, feature_part, 0)

    def part_a(zb):
        return ut[:, lanes(wrap(zb, NZ) * 128, 128)]

    def part_b(yb):
        return ut[:, lanes(GROUP // 2 + wrap(yb, NY) * 256, 256)]

    def step_a(s):
        plus = part_a(z + 4 - s)
        if s:
            arrived(rap.at[s - 1], RSAP + s - 1)
            plus = plus + rap[s - 1].astype(F32)
        sap[s] = plus.astype(BF16)
        push(sap.at[s], rap.at[s], RSAP + s, up_z)
        if s < 3:
            minus = part_a(z - 3 + s)
            if s:
                arrived(ram.at[s - 1], RSAM + s - 1)
                minus = minus + ram[s - 1].astype(F32)
            sam[s] = minus.astype(BF16)
            push(sam.at[s], ram.at[s], RSAM + s, down_z)

    def step_b(s):
        plus = part_b(y + 2 - s)
        if s:
            arrived(rbp.at[s - 1], RSBP + s - 1)
            plus = plus + rbp[s - 1].astype(F32)
        sbp[s] = plus.astype(BF16)
        push(sbp.at[s], rbp.at[s], RSBP + s, up_y)
        if s == 0:
            sbm[0] = part_b(y - 1).astype(BF16)
            push(sbm.at[0], rbm.at[0], RSBM, down_y)

    step_a(0)
    step_b(0)
    step_a(1)
    step_a(2)
    step_b(1)
    step_a(3)
    arrived(ram.at[2], RSAM + 2)
    arrived(rap.at[3], RSAP + 3)
    slab = part_a(z) + rap[3].astype(F32) + ram[2].astype(F32)
    wa[...] = slab.T
    wab[...] = wa[...].astype(BF16)
    for k, off in enumerate(xy):
        px, py = xy_to(*off)
        piece = rows16((px * NY + py) * HALF, HALF)
        push(wab.at[piece, :], r2a.at[k], RS2A + k, at(px, py, z))
    arrived(rbm.at[0], RSBM)
    arrived(rbp.at[1], RSBP + 1)
    slab = part_b(y) + rbp[1].astype(F32) + rbm[0].astype(F32)
    wb[...] = slab.T
    wbb[...] = wb[...].astype(BF16)
    for k, off in enumerate(xz):
        px, pz = xz_to(*off)
        piece = rows16((px * NZ + pz) * HALF, HALF)
        push(wbb.at[piece, :], r2b.at[k], RS2B + k, at(px, y, pz))

    for i in range(NCB):
        arrived(xrecv.at[i], XLO + i)
        both = xsend[i].astype(F32) + xrecv[i].astype(F32)
        place = gsum.at[rows16(mine + i * SB, SB), :]
        gsum[rows16(mine + i * SB, SB), :] = both.astype(BF16)
        push(place, place, CORE2 + i, core_peer)

    def update(first):
        part = pl.ds(pl.multiple_of(first, SB), SB)
        rows = crow[part, :].astype(F32)
        norm = row_norm(rows)
        unit_c = rows / norm
        grad = gsum[part, :].astype(F32)
        step = (grad - unit_c * jnp.sum(unit_c * grad, axis=1, keepdims=True)) / norm
        new_m = MOMENT_RATE * momg[part, :] + step
        newm_ref[part, :] = new_m
        newc_ref[part, :] = (rows - LEARN_RATE * new_m).astype(BF16)

    for i in range(NCB):
        update(mine + i * SB)

    for k in range(7):
        arrived(r2a.at[k], RS2A + k)
    g_a = wa[pl.ds(pl.multiple_of((x * NY + y) * HALF, HALF), HALF), :]
    g_a = g_a + sum(r2a[k].astype(F32) for k in range(7))
    for k in range(15):
        arrived(r2b.at[k], RS2B + k)
    g_b = wb[pl.ds(pl.multiple_of((x * NZ + z) * HALF, HALF), HALF), :]
    g_b = g_b + sum(r2b[k].astype(F32) for k in range(15))
    for h, grad in enumerate((g_a, g_b)):
        own = feat_ref[h * HALF : (h + 1) * HALF, :].astype(F32)
        norm = row_norm(own)
        unit_f = own / norm
        dot = jnp.sum(unit_f * grad, axis=1, keepdims=True)
        fgrad_ref[h * HALF : (h + 1) * HALF, :] = (grad - unit_f * dot) / norm

    for i in range(NCB):
        arrived(gsum.at[rows16(other + i * SB, SB), :], CORE2 + i)
        update(other + i * SB)

    for copy in pending:
        copy.wait_send()


def local(features, centers, momentum, sample_rows, labels):
    cls = lax.axis_index("cls")
    x, y, z = cls // (NY * NZ), cls // NZ % NY, cls % NZ
    ids = jnp.broadcast_to((sample_rows + cls * ROWS)[:, None], (SLOTS, LANES))
    place = jnp.arange(GROUP // HALF, dtype=jnp.int32)
    at_a = z * 8 + x * NY + y
    at_b = GROUP // TOK + y * 16 + x * NZ + z
    placed = jnp.where(
        (place == at_a)[:, None],
        labels[None, :HALF],
        jnp.where((place == at_b)[:, None], labels[None, HALF:], 0),
    ).reshape(16, LANES)

    vm = pl.BlockSpec(memory_space=pltpu.VMEM)
    hbm = pl.BlockSpec(memory_space=pl.ANY)
    v = pltpu.VMEM
    f_grad, loss, new_c, new_m = pl.pallas_call(
        kernel,
        out_shape=(
            jax.ShapeDtypeStruct((TOK, D), F32),
            jax.ShapeDtypeStruct((16, LANES), F32),
            jax.ShapeDtypeStruct((SLOTS, D), BF16),
            jax.ShapeDtypeStruct((SLOTS, D), F32),
        ),
        in_specs=[vm, vm, vm, pl.BlockSpec(memory_space=pltpu.SMEM), hbm, hbm],
        out_specs=(vm, vm, vm, vm),
        scratch_shapes=[
            v((ROWS, D), BF16), v((ROWS, D), F32), v((GROUP, D), BF16),
            v((SLOTS, D), BF16), v((SLOTS, D), BF16), v((D, SLOTS), BF16), v((SLOTS, D), F32),
            v((SLOTS, GROUP), F32), v((SLOTS, GROUP), BF16), v((D, GROUP), F32),
            v((16, LANES), jnp.int32), v((7, 16, LANES), jnp.int32), v((16, LANES), jnp.int32),
            v((7, 16, LANES), jnp.int32),
            v((32, LANES), F32), v((7, 32, LANES), F32), v((32, LANES), F32), v((7, 32, LANES), F32),
            v((16, LANES), F32),
            v((NCB, SB, D), BF16), v((NCB, SB, D), BF16), v((NCB, SB, D), BF16),
            v((NCB, SB, D), BF16), v((NCB, SB, D), BF16), v((SLOTS, D), BF16),
            v((4, D, 128), BF16), v((4, D, 128), BF16), v((3, D, 128), BF16), v((3, D, 128), BF16),
            v((2, D, 256), BF16), v((2, D, 256), BF16), v((1, D, 256), BF16), v((1, D, 256), BF16),
            v((128, D), F32), v((256, D), F32), v((128, D), BF16), v((256, D), BF16),
            v((7, HALF, D), BF16), v((15, HALF, D), BF16),
            pltpu.SemaphoreType.DMA((N_SEMS,)), pltpu.SemaphoreType.DMA((N_SEMS,)),
            pltpu.SemaphoreType.DMA((2,)),
        ],
        compiler_params=pltpu.CompilerParams(
            collective_id=0, has_side_effects=True, vmem_limit_bytes=60 * 1024 * 1024
        ),
    )(features, ids, placed, sample_rows, centers, momentum)
    flat = loss.reshape(GROUP // HALF, HALF)
    own = jnp.concatenate(
        [
            lax.dynamic_slice_in_dim(flat, at_a, 1),
            lax.dynamic_slice_in_dim(flat, at_b, 1),
        ],
        axis=0,
    ).reshape(TOK)
    return (f_grad, own, new_c, new_m)


def solution(mesh):
    in_specs = (
        P(("rep", "cls"), None),
        P("cls", None),
        P("cls", None),
        P("cls"),
        P(("rep", "cls")),
    )
    out_specs = (P(("rep", "cls"), None), P(("rep", "cls")), P("cls", None), P("cls", None))
    return jax.shard_map(local, mesh=mesh, in_specs=in_specs, out_specs=out_specs, check_vma=False)
```

time: 943 us -> 116 us (0.12)
  waiting for transfers between devices: 481 us -> 0 us
  blocking collectives: 383 us -> 0 us
  Pallas kernels: 0 us -> 103 us
  matrix products: 23.6 us -> 0 us
  other arithmetic: 23.2 us -> 1.34 us
  between operations: 14.5 us -> 0.76 us
    reduce_scatter x1 -> x0, waiting for transfers between devices: 366 us -> none  [local(): lax.psum_scatter(logit_scale * jnp.dot(soft, cent_bf, preferred_element_t...]
    psum x1 -> x0, blocking collectives: 356 us -> none  [local(): lax.psum((jnp.sum(expo, axis=1), jnp.sum(matches * logits, axis=1)), 'cls')]
    pallas_call x0 -> x1, Pallas kernels: none -> 103 us  [local(): pl.pallas_call(kernel, out_shape=(jax.ShapeDtypeStruct((TOK, D), F32), ja...]
    all_gather x1 -> x0, waiting for transfers between devices: 85.4 us -> none  [local(): lax.all_gather(feat_bf, 'cls', axis=0, tiled=True)]
    psum x1 -> x0, waiting for transfers between devices: 29.3 us -> none  [local(): lax.psum(grad_local.astype(jnp.bfloat16), 'rep').astype(jnp.float32)]
    unnamed x1 -> x0, blocking collectives: 27.8 us -> none
    dot_general x3 -> x0, matrix products: 23.6 us -> none  [the longest x1 10.2 us: local(): lax.dot_general(gathered, cent_bf, (((1,), (1,)), ((), ())), preferred_el...]
    gather x2 -> x0, local copies, waits for them, and re-layouts: 13.3 us -> none  [the longest x1 7.88 us: local(): moment_rows = jnp.take(momentum, sample_rows, axis=0)]
  transfers between devices with their start and end apart: 3 -> 0, of which waited for: 3 -> 0; matrix products, arithmetic and copies ran while one was open for 4% -> 0% of each run, Pallas kernels for 0% -> 0%
where the time goes in v1:
time: 116 us; the launch traced here: 115 us
  Pallas kernels  103 us (89%)
  local copies, waits for them, and re-layouts  9.79 us (8%)
  other arithmetic  1.34 us (1%)
    pallas_call x1, Pallas kernels, local(): pl.pallas_call(kernel, out_shape=(jax.ShapeDtypeStruct((TOK, D), F32), ja...  103 us
    unnamed x5, local copies, waits for them, and re-layouts  5.79 us

profile of v1, /device:TPU:2, one launch (start us, length us, event | category | flops | bytes accessed | tf_op | source)
XLA Modules:
  0.0 115.2 jit_solution(1498049348470028317)
XLA Ops:
  0.7 0.8 fusion.2
  1.5 0.1 broadcast_in_dim.62
  1.6 0.1 broadcast_in_dim.67
  1.7 0.7 broadcast_add_fusion
  2.4 0.1 broadcast_in_dim.64
  2.5 0.1 broadcast_in_dim.65
  2.6 0.1 broadcast_in_dim.59
  2.7 0.1 broadcast_in_dim.60
  2.8 0.6 select_select_fusion.lab_ref
  3.4 1.1 broadcast_in_dim.58.ids_ref
  4.5 103.3 %shard_map.84 = (f32[32,512]{1,0:T(8,128)}, f32[16,128]{1,0:T(8,128)}, bf16[1536,512]{1,0:T(8,128)(2,1)}, f32[1536,512]{1,0:T(8,128)}) custom-call(bf16[32,512]{1,0:T(8,128)(2,1)} %feat_ref.1, s32[1536,128]{1,0:T(8,128)} %broadcast_in_dim.58.ids_ref, s32[16,128]{1,0:T(8,128)} %select_select_fusion.lab_ref, s32[1536]{0:T(1024)} %rows_ref.1, ...), custom_call_target="tpu_custom_call" | custom-call | tf_op jit(solution)/shard_map/pallas_call | solution.py:449
  107.8 0.0 copy-start
  107.8 0.9 reshape.34
  108.8 0.6 reshape.35
  109.4 1.5 %copy.12 = f32[32,512]{1,0:T(8,128)} copy(f32[32,512]{1,0:T(8,128)} %get-tuple-element.20) | data formatting | bytes 131072
  110.9 2.7 %copy.13 = bf16[1536,512]{1,0:T(8,128)(2,1)} copy(bf16[1536,512]{1,0:T(8,128)(2,1)} %get-tuple-element.22) | data formatting | bytes 3145728
  113.5 0.0 copy-done
  113.5 1.7 %copy.14 = f32[1536,512]{1,0:T(8,128)} copy(f32[1536,512]{1,0:T(8,128)S(1)} %copy-done) | data formatting | bytes 6291456
  (6 shorter events, 0.0 us)
Async XLA Ops:
  107.8 5.7 %copy-start = (f32[1536,512]{1,0:T(8,128)S(1)}, f32[1536,512]{1,0:T(8,128)}, u32[]{:S(2)}) copy-start(f32[1536,512]{1,0:T(8,128)} %get-tuple-element.23) | copy-start | bytes 9437188

commit v2 on v1

v2 whole, which is shorter than its diff:
```python
import math

import jax
import jax.numpy as jnp
from jax import lax
from jax.experimental import pallas as pl
from jax.experimental.pallas import tpu as pltpu
from jax.sharding import PartitionSpec as P

MESH = pl.DeviceIdType.MESH

EPS = 1e-06
SCALE = 64.0
MARGIN = 0.35
MOMENT_RATE = 0.9
LEARN_RATE = 0.1

NX, NY, NZ = 2, 4, 8
TOK = 32
HALF = TOK // 2
GROUP = TOK * NX * NY * NZ
D = 512
SLOTS = 1536
ROWS = 2048
SB = 256
NSB = SLOTS // SB
OWN = SLOTS // 2
NCB = OWN // SB
LANES = 128
LOG2E = math.log2(math.e)
F32, BF16 = jnp.float32, jnp.bfloat16


class Sems:
    def __init__(self):
        self.n = 0

    def take(self, count):
        first = self.n
        self.n += count
        return first


_s = Sems()
AG1A, AG1B, AG2B = _s.take(7), _s.take(7), _s.take(7)
AGAP, AGAM = _s.take(4), _s.take(3)
LAB1, LAB2, TOT1, TOT2, POS1, POS2 = (_s.take(7) for _ in range(6))
CORE1, XLO, CORE2 = _s.take(3), _s.take(3), _s.take(3)
RSAP, RSAM, RSB = _s.take(4), _s.take(3), _s.take(3)
RS2A, RSBX, RSBZ = _s.take(7), _s.take(1), _s.take(7)
N_SEMS = _s.n


def wrap(value, n):
    return lax.rem(value + n, n)


def rows16(start, count):
    return pl.ds(pl.multiple_of(start, 16), count)


def lanes(start, count):
    return pl.ds(pl.multiple_of(start, LANES), count)


def row_norm(floats):
    return jnp.sqrt(jnp.sum(floats * floats, axis=-1, keepdims=True) + EPS)


def kernel(
    feat_ref, rowv_ref, lab_ref, rows_ref, cent_hbm, mom_hbm,
    fgrad_ref, loss_ref, crow_hbm, momg_hbm, gsum_hbm,
    cent_v, mom_v, feats, ids_ref, crow, cbf, cbt, momg, expo, soft,
    place, labs, lab1, lab1s, lab2, tot, tot1, tot1s, tot2, rtot, pos1, pos1s, pos2,
    csend, cown, crecv, xsend, xrecv, gown,
    ua, ub, sap, rap, sam, ram, sb_, rb_,
    wa, wb, wab, wbb, wbz, wbzb, r2a, rbx, rbz,
    ssem, rsem, lsem,
):
    rep, cls = lax.axis_index("rep"), lax.axis_index("cls")
    x, y, z = lax.div(cls, NY * NZ), lax.rem(lax.div(cls, NZ), NY), lax.rem(cls, NZ)
    x_lo, core = lax.div(rep, 2), lax.rem(rep, 2)

    def at(x, y, z):
        return (rep, (x * NY + y) * NZ + z)

    xy = [(k % NX, k // NX) for k in range(1, NX * NY)]

    def flip(dx):
        return x if dx == 0 else 1 - x

    def xy_to(k):
        dx, dy = xy[k]
        return flip(dx), wrap(y + dy, NY)

    def xy_from(k):
        dx, dy = xy[k]
        return flip(dx), wrap(y - dy, NY)

    def z_to(k):
        return wrap(z + k + 1, NZ)

    def z_from(k):
        return wrap(z - k - 1, NZ)

    xy_peers = [at(*xy_to(k), z) for k in range(7)]
    z_peers = [at(x, y, z_to(k)) for k in range(7)]
    y_peers = [at(x, wrap(y + k + 1, NY), z) for k in range(3)]
    x_peer = at(1 - x, y, z)
    core_peer = (x_lo * 2 + 1 - core, cls)
    xlo_peer = ((1 - x_lo) * 2 + core, cls)
    up_z, down_z = z_peers[0], z_peers[6]

    pending = []

    def push(src, dst, sem, device):
        copy = pltpu.make_async_remote_copy(
            src_ref=src, dst_ref=dst, send_sem=ssem.at[sem], recv_sem=rsem.at[sem],
            device_id=device, device_id_type=MESH,
        )
        copy.start()
        pending.append(copy)

    def arrived(dst, sem):
        pltpu.make_async_remote_copy(
            src_ref=dst, dst_ref=dst, send_sem=ssem.at[sem], recv_sem=rsem.at[sem],
            device_id=core_peer, device_id_type=MESH,
        ).wait_recv()

    stores = []

    def store(src, dst, sem):
        copy = pltpu.make_async_copy(src, dst, lsem.at[sem])
        copy.start()
        stores.append(copy)

    barrier = pltpu.get_barrier_semaphore()
    greet = xy_peers + z_peers + [core_peer, xlo_peer]
    for device in greet:
        pl.semaphore_signal(barrier, inc=1, device_id=device, device_id_type=MESH)

    load_c = pltpu.make_async_copy(cent_hbm, cent_v, lsem.at[0])
    load_m = pltpu.make_async_copy(mom_hbm, mom_v, lsem.at[1])
    load_c.start()
    load_m.start()

    half = GROUP // 2
    my_q, my_b = x * NY + y, y * NX + x

    floats = feat_ref[...].astype(F32)
    unit = (floats / row_norm(floats)).astype(BF16)
    own_a = rows16(z * 128 + my_q * HALF, HALF)
    own_b = rows16(half + my_b * 128 + z * HALF, HALF)
    feats[own_a, :] = unit[:HALF]
    feats[own_b, :] = unit[HALF:]

    lane = lax.broadcasted_iota(jnp.int32, (8, LANES), 1)
    row = lax.broadcasted_iota(jnp.int32, (8, LANES), 0)
    lab_a = jnp.broadcast_to(lab_ref[0:1, :], (8, LANES))
    lab_b = jnp.broadcast_to(lab_ref[1:2, :], (8, LANES))
    place[0:8, :] = jnp.where((row == z) & (lane // HALF == my_q), lab_a, 0)
    place[8:16, :] = jnp.where((row == my_b) & (lane // HALF == z), lab_b, 0)

    pl.semaphore_wait(barrier, len(greet))

    for k in range(7):
        push(feats.at[own_a, :], feats.at[own_a, :], AG1A + k, xy_peers[k])
    for k in range(7):
        push(feats.at[own_b, :], feats.at[own_b, :], AG1B + k, z_peers[k])
    for k in range(7):
        push(place, lab1.at[k], LAB1 + k, xy_peers[k])

    for b in range(SLOTS // LANES):
        wide = jnp.broadcast_to(rowv_ref[b : b + 1, :].astype(F32), (LANES, LANES))
        ids_ref[b * LANES : (b + 1) * LANES, :] = wide.T.astype(jnp.int32) + cls * ROWS

    load_c.wait()

    def pick(sb):
        part = slice(sb * SB, (sb + 1) * SB)
        ids = ids_ref[part, :] - cls * ROWS
        col = lax.broadcasted_iota(jnp.int32, (SB, LANES), 1)
        hot = jnp.concatenate(
            [jnp.where(ids == col + j * LANES, 1.0, 0.0).astype(BF16) for j in range(ROWS // LANES)],
            axis=1,
        )
        got = jnp.dot(hot, cent_v[...], preferred_element_type=F32)
        crow[part, :] = got.astype(BF16)
        cbf[part, :] = (got / row_norm(got)).astype(BF16)

    for sb in range(NSB // 2):
        pick(sb)

    def blk_a(zb):
        return feats.at[rows16(zb * 128, 128), :]

    def blk_b(px, py):
        return feats.at[rows16(half + (py * NX + px) * 128, 128), :]

    for k in range(7):
        px, py = xy_from(k)
        arrived(feats.at[rows16(z * 128 + (px * NY + py) * HALF, HALF), :], AG1A + k)
    push(blk_a(z), blk_a(z), AGAP, up_z)
    push(blk_a(z), blk_a(z), AGAM, down_z)
    for k in range(7):
        arrived(feats.at[rows16(half + my_b * 128 + z_from(k) * HALF, HALF), :], AG1B + k)
    for k in range(7):
        push(blk_b(x, y), blk_b(x, y), AG2B + k, xy_peers[k])

    for k in range(7):
        arrived(lab1.at[k], LAB1 + k)
    lab1s[...] = place[...] + sum(lab1[k] for k in range(7))
    for k in range(7):
        push(lab1s, lab2.at[k], LAB2 + k, z_peers[k])

    for sb in range(NSB // 2, NSB):
        pick(sb)
    store(crow, crow_hbm, 2)

    for k in range(7):
        arrived(lab2.at[k], LAB2 + k)
    labs[...] = lab1s[...] + sum(lab2[k] for k in range(7))

    def logits(tiles):
        block = jnp.concatenate([feats[rows16(t * LANES, LANES), :] for t in tiles], axis=0)
        rows = [labs[pl.ds(t, 1), :] for t in tiles]
        sums = [jnp.zeros((8, LANES), F32) for _ in range(4)]
        for sb in range(NSB):
            part = slice(sb * SB, (sb + 1) * SB)
            cosine = lax.dot_general(
                cbf[part, :], block, (((1,), (1,)), ((), ())), preferred_element_type=F32
            )
            ids = ids_ref[part, :]
            for h, t in enumerate(tiles):
                cos_h = cosine[:, h * LANES : (h + 1) * LANES]
                match = ids == rows[h]
                logit = SCALE * (cos_h - jnp.where(match, MARGIN, 0.0))
                e = jnp.exp2((logit - SCALE) * LOG2E)
                expo[part, lanes(t * LANES, LANES)] = e
                sums[h] += jnp.sum(e.reshape(SB // 8, 8, LANES), axis=0)
                hit = jnp.where(match, logit, 0.0)
                sums[2 + h] += jnp.sum(hit.reshape(SB // 8, 8, LANES), axis=0)
        for h, t in enumerate(tiles):
            tot[pl.ds(t, 1), :] = jnp.sum(sums[h], axis=0, keepdims=True)
            tot[pl.ds(16 + t, 1), :] = jnp.sum(sums[2 + h], axis=0, keepdims=True)

    def ring(s):
        zp, zm = wrap(z - 1 - s, NZ), wrap(z + 1 + s, NZ)
        arrived(blk_a(zp), AGAP + s)
        if s < 3:
            push(blk_a(zp), blk_a(zp), AGAP + s + 1, up_z)
            arrived(blk_a(zm), AGAM + s)
        if s < 2:
            push(blk_a(zm), blk_a(zm), AGAM + s + 1, down_z)
        return zp, zm

    def plane(k):
        px, py = xy_from(k)
        arrived(blk_b(px, py), AG2B + k)
        return 8 + py * NX + px

    logits((z, 8 + my_b))
    logits(ring(0))
    logits(ring(1))
    logits((plane(0), plane(1)))
    logits((plane(2), plane(3)))
    logits(ring(2))
    logits((plane(4), plane(5)))
    logits((ring(3)[0], plane(6)))

    t_all, p_all = tot.at[0:16, :], tot.at[16:32, :]
    for k in range(7):
        push(t_all, tot1.at[k], TOT1 + k, xy_peers[k])
    for k in range(7):
        push(p_all, pos1.at[k], POS1 + k, xy_peers[k])

    load_m.wait()

    def pick_m(j, carry):
        for u in range(16):
            i = j * 16 + u
            momg[pl.ds(i, 1), :] = mom_v[pl.ds(rows_ref[i], 1), :]
        return carry

    lax.fori_loop(0, SLOTS // 32, pick_m, 0)
    for k in range(7):
        arrived(tot1.at[k], TOT1 + k)
    tot1s[...] = tot[0:16, :] + sum(tot1[k] for k in range(7))
    for k in range(7):
        push(tot1s, tot2.at[k], TOT2 + k, z_peers[k])
    for k in range(7):
        arrived(pos1.at[k], POS1 + k)
    pos1s[...] = tot[16:32, :] + sum(pos1[k] for k in range(7))
    for k in range(7):
        push(pos1s, pos2.at[k], POS2 + k, z_peers[k])

    lax.fori_loop(SLOTS // 32, SLOTS // 16, pick_m, 0)
    store(momg, momg_hbm, 3)
    for sb in range(NSB):
        cbt[:, sb * SB : (sb + 1) * SB] = cbf[sb * SB : (sb + 1) * SB, :].T

    for k in range(7):
        arrived(tot2.at[k], TOT2 + k)
    totals = tot1s[...] + sum(tot2[k] for k in range(7))
    rtot[...] = 1.0 / totals

    def soften(tiles):
        for t in tiles:
            col = lanes(t * LANES, LANES)
            inverse, lab = rtot[pl.ds(t, 1), :], labs[pl.ds(t, 1), :]
            for sb in range(NSB):
                part = slice(sb * SB, (sb + 1) * SB)
                value = expo[part, col] * inverse
                match = jnp.where(ids_ref[part, :] == lab, 1.0, 0.0)
                soft[part, col] = (value - match).astype(BF16)

    def feature_part(tiles):
        cols = jnp.concatenate([soft[:, lanes(t * LANES, LANES)] for t in tiles], axis=1)
        return SCALE * jnp.dot(cbt[...], cols, preferred_element_type=F32)

    def center_grad(first):
        part = pl.ds(pl.multiple_of(first, SB), SB)
        return (SCALE * jnp.dot(soft[part, :], feats[...], preferred_element_type=F32)).astype(BF16)

    mine, other = core * OWN, (1 - core) * OWN

    def grad_other(i):
        csend[i] = center_grad(other + i * SB)
        push(csend.at[i], crecv.at[i], CORE1 + i, core_peer)

    def grad_mine(i):
        cown[i] = center_grad(mine + i * SB)

    def join_cores(i):
        arrived(crecv.at[i], CORE1 + i)
        xsend[i] = (cown[i].astype(F32) + crecv[i].astype(F32)).astype(BF16)
        push(xsend.at[i], xrecv.at[i], XLO + i, xlo_peer)

    def tiles_a(s):
        return wrap(z + 4 - s, NZ), wrap(z - 3 + s, NZ)

    def tiles_b(yb):
        return 8 + yb * NX, 8 + yb * NX + 1

    def ring_sum(s):
        plus = ua[s][:, :128]
        if s:
            arrived(rap.at[s - 1], RSAP + s - 1)
            plus = plus + rap[s - 1].astype(F32)
        sap[s] = plus.astype(BF16)
        push(sap.at[s], rap.at[s], RSAP + s, up_z)
        if s < 3:
            minus = ua[s][:, 128:]
            if s:
                arrived(ram.at[s - 1], RSAM + s - 1)
                minus = minus + ram[s - 1].astype(F32)
            sam[s] = minus.astype(BF16)
            push(sam.at[s], ram.at[s], RSAM + s, down_z)

    def part_a(s):
        ua[s] = feature_part(tiles_a(s))

    soften(tiles_a(0))
    part_a(0)
    ring_sum(0)
    y_to = [wrap(y + k + 1, NY) for k in range(3)]
    for k in (1, 0, 2):
        soften(tiles_b(y_to[k]))
        sb_[k] = feature_part(tiles_b(y_to[k])).astype(BF16)
        push(sb_.at[k], rb_.at[k], RSB + k, y_peers[k])
    soften(tiles_a(1))
    soften(tiles_a(2))
    soften(tiles_a(3))
    soften(tiles_b(y))
    grad_other(0)
    grad_mine(0)
    part_a(1)
    ring_sum(1)
    grad_other(1)
    join_cores(0)
    grad_mine(1)
    grad_other(2)
    join_cores(1)
    grad_mine(2)
    part_a(2)
    ring_sum(2)
    join_cores(2)
    part_a(3)
    ub[...] = feature_part(tiles_b(y))

    for k in range(7):
        arrived(pos2.at[k], POS2 + k)
    positive = pos1s[...] + sum(pos2[k] for k in range(7))
    loss_ref[...] = jnp.log(totals) + SCALE - positive

    ring_sum(3)

    for k in range(3):
        arrived(rb_.at[k], RSB + k)
    slab = ub[...] + sum(rb_[k].astype(F32) for k in range(3))
    wb[...] = slab.T
    wbb[...] = wb[rows16((1 - x) * 128, 128), :].astype(BF16)
    push(wbb, rbx, RSBX, x_peer)

    arrived(ram.at[2], RSAM + 2)
    arrived(rap.at[3], RSAP + 3)
    slab = ua[3][:, 128:] + rap[3].astype(F32) + ram[2].astype(F32)
    wa[...] = slab.T
    wab[...] = wa[...].astype(BF16)
    for k in range(7):
        px, py = xy_to(k)
        push(wab.at[rows16((px * NY + py) * HALF, HALF), :], r2a.at[k], RS2A + k, xy_peers[k])

    arrived(rbx, RSBX)
    wbz[...] = wb[rows16(x * 128, 128), :] + rbx[...].astype(F32)
    wbzb[...] = wbz[...].astype(BF16)
    for k in range(7):
        push(wbzb.at[rows16(z_to(k) * HALF, HALF), :], rbz.at[k], RSBZ + k, z_peers[k])

    for i in range(NCB):
        arrived(xrecv.at[i], XLO + i)
        gown[i] = (xsend[i].astype(F32) + xrecv[i].astype(F32)).astype(BF16)
        place_i = gsum_hbm.at[rows16(mine + i * SB, SB), :]
        push(gown.at[i], place_i, CORE2 + i, core_peer)
        store(gown.at[i], place_i, 4 + i)

    for k in range(7):
        arrived(r2a.at[k], RS2A + k)
    g_a = wa[rows16(my_q * HALF, HALF), :] + sum(r2a[k].astype(F32) for k in range(7))
    for k in range(7):
        arrived(rbz.at[k], RSBZ + k)
    g_b = wbz[rows16(z * HALF, HALF), :] + sum(rbz[k].astype(F32) for k in range(7))
    for h, grad in enumerate((g_a, g_b)):
        own = feat_ref[h * HALF : (h + 1) * HALF, :].astype(F32)
        norm = row_norm(own)
        unit_f = own / norm
        dot = jnp.sum(unit_f * grad, axis=1, keepdims=True)
        fgrad_ref[h * HALF : (h + 1) * HALF, :] = (grad - unit_f * dot) / norm

    for i in range(NCB):
        arrived(gsum_hbm.at[rows16(other + i * SB, SB), :], CORE2 + i)
    for copy in pending:
        copy.wait_send()
    for copy in stores:
        copy.wait()


def update(crow_ref, momg_ref, gsum_ref, fgrad_ref, loss_ref, newc_ref, newm_ref, fout_ref, lout_ref):
    rows = crow_ref[...].astype(F32)
    norm = row_norm(rows)
    unit = rows / norm
    grad = gsum_ref[...].astype(F32)
    step = (grad - unit * jnp.sum(unit * grad, axis=1, keepdims=True)) / norm
    new_m = MOMENT_RATE * momg_ref[...] + step
    newm_ref[...] = new_m
    newc_ref[...] = (rows - LEARN_RATE * new_m).astype(BF16)
    fout_ref[...] = fgrad_ref[...]
    lout_ref[...] = loss_ref[...]


def local(features, centers, momentum, sample_rows, labels):
    vm = pl.BlockSpec(memory_space=pltpu.VMEM)
    hbm = pl.BlockSpec(memory_space=pl.ANY)
    v = pltpu.VMEM
    sds = jax.ShapeDtypeStruct
    f_grad, loss, crow, momg, gsum = pl.pallas_call(
        kernel,
        out_shape=(
            sds((TOK, D), F32),
            sds((16, LANES), F32),
            sds((SLOTS, D), BF16),
            sds((SLOTS, D), F32),
            sds((SLOTS, D), BF16),
        ),
        in_specs=[vm, vm, vm, pl.BlockSpec(memory_space=pltpu.SMEM), hbm, hbm],
        out_specs=(vm, vm, hbm, hbm, hbm),
        scratch_shapes=[
            v((ROWS, D), BF16), v((ROWS, D), F32), v((GROUP, D), BF16), v((SLOTS, LANES), jnp.int32),
            v((SLOTS, D), BF16), v((SLOTS, D), BF16), v((D, SLOTS), BF16), v((SLOTS, D), F32),
            v((SLOTS, GROUP), F32), v((SLOTS, GROUP), BF16),
            v((16, LANES), jnp.int32), v((16, LANES), jnp.int32), v((7, 16, LANES), jnp.int32),
            v((16, LANES), jnp.int32), v((7, 16, LANES), jnp.int32),
            v((32, LANES), F32), v((7, 16, LANES), F32), v((16, LANES), F32), v((7, 16, LANES), F32),
            v((16, LANES), F32), v((7, 16, LANES), F32), v((16, LANES), F32), v((7, 16, LANES), F32),
            v((NCB, SB, D), BF16), v((NCB, SB, D), BF16), v((NCB, SB, D), BF16),
            v((NCB, SB, D), BF16), v((NCB, SB, D), BF16), v((NCB, SB, D), BF16),
            v((4, D, 256), F32), v((D, 256), F32),
            v((4, D, 128), BF16), v((4, D, 128), BF16), v((3, D, 128), BF16), v((3, D, 128), BF16),
            v((3, D, 256), BF16), v((3, D, 256), BF16),
            v((128, D), F32), v((256, D), F32), v((128, D), BF16), v((128, D), BF16),
            v((128, D), F32), v((128, D), BF16),
            v((7, HALF, D), BF16), v((128, D), BF16), v((7, HALF, D), BF16),
            pltpu.SemaphoreType.DMA((N_SEMS,)), pltpu.SemaphoreType.DMA((N_SEMS,)),
            pltpu.SemaphoreType.DMA((4 + NCB,)),
        ],
        compiler_params=pltpu.CompilerParams(
            collective_id=0, has_side_effects=True, vmem_limit_bytes=60 * 1024 * 1024
        ),
    )(
        features,
        sample_rows.reshape(SLOTS // LANES, LANES),
        jnp.tile(labels.reshape(2, HALF), (1, LANES // HALF)),
        sample_rows,
        centers,
        momentum,
    )
    def rows_of(i):
        return (i, 0)

    def whole(i):
        return (0, 0)

    block = pl.BlockSpec((SB, D), rows_of)
    new_c, new_m, f_grad, loss = pl.pallas_call(
        update,
        grid=(NSB,),
        out_shape=(
            sds((SLOTS, D), BF16), sds((SLOTS, D), F32), sds((TOK, D), F32), sds((16, LANES), F32),
        ),
        in_specs=[block, block, block, pl.BlockSpec((TOK, D), whole), pl.BlockSpec((16, LANES), whole)],
        out_specs=(block, block, pl.BlockSpec((TOK, D), whole), pl.BlockSpec((16, LANES), whole)),
    )(crow, momg, gsum, f_grad, loss)
    cls = lax.axis_index("cls")
    x, y, z = cls // (NY * NZ), cls // NZ % NY, cls % NZ
    flat = loss.reshape(GROUP // HALF, HALF)
    own = jnp.concatenate(
        [
            lax.dynamic_slice_in_dim(flat, z * 8 + x * NY + y, 1),
            lax.dynamic_slice_in_dim(flat, GROUP // TOK + (y * NX + x) * 8 + z, 1),
        ],
        axis=0,
    ).reshape(TOK)
    return (f_grad, own, new_c, new_m)


def solution(mesh):
    in_specs = (
        P(("rep", "cls"), None),
        P("cls", None),
        P("cls", None),
        P("cls"),
        P(("rep", "cls")),
    )
    out_specs = (P(("rep", "cls"), None), P(("rep", "cls")), P("cls", None), P("cls", None))
    return jax.shard_map(local, mesh=mesh, in_specs=in_specs, out_specs=out_specs, check_vma=False)
```

time: 116 us -> 99.5 us (0.86)
  Pallas kernels: 103 us -> 95.6 us
  local copies, waits for them, and re-layouts: 9.79 us -> 2.76 us
  other arithmetic: 1.34 us -> 0.01 us
    pallas_call x1 -> x2, Pallas kernels: 103 us -> 95.6 us  [the longest x1 88.4 us: local(): pl.pallas_call(kernel, out_shape=(sds((TOK, D), F32), sds((16, LANES), F3...]
    unnamed x5 -> x0, local copies, waits for them, and re-layouts: 5.79 us -> none
    broadcast_in_dim x9 -> x0, local copies, waits for them, and re-layouts: 1.67 us -> none  [the longest x1 1.15 us: local(): ids = jnp.broadcast_to((sample_rows + cls * ROWS)[:, None], (SLOTS, LANES))]
    another operation x0 -> x3, local copies, waits for them, and re-layouts: none -> 1.39 us  [local(): jnp.tile(labels.reshape(2, HALF), (1, LANES // HALF))]
where the time goes in v2:
time: 99.5 us; the launch traced here: 99.1 us
  Pallas kernels  95.6 us (96%)
  local copies, waits for them, and re-layouts  2.76 us (3%)
    pallas_call x1, Pallas kernels, local(): pl.pallas_call(kernel, out_shape=(sds((TOK, D), F32), sds((16, LANES), F3...  88.4 us
    pallas_call x1, Pallas kernels, local(): pl.pallas_call(update, grid=(NSB,), out_shape=(sds((SLOTS, D), BF16), sds...  7.23 us

profile of v2, /device:TPU:2, one launch (start us, length us, event | category | flops | bytes accessed | tf_op | source)
XLA Modules:
  0.0 99.1 jit_solution(13075140789702409231)
XLA Ops:
  0.6 0.7 tile.10
  1.4 0.6 tile.12.lab_ref
  2.0 88.4 %shard_map.84 = (f32[32,512]{1,0:T(8,128)}, f32[16,128]{1,0:T(8,128)}, bf16[1536,512]{1,0:T(8,128)(2,1)}, f32[1536,512]{1,0:T(8,128)}, bf16[1536,512]{1,0:T(8,128)(2,1)}) custom-call(bf16[32,512]{1,0:T(8,128)(2,1)} %feat_ref.1, s32[12,128]{1,0:T(8,128)} %bitcast.1, s32[2,128]{1,0:T(2,128)} %tile.12.lab_ref, s32[1536]{0:T(1024)} %rows_ref.1, ...), custom_call_target="tpu_custom_call" | custom-call | tf_op jit(solution)/shard_map/pallas_call | solution.py:466
  90.4 7.2 %shard_map.85 = (bf16[1536,512]{1,0:T(8,128)(2,1)}, f32[1536,512]{1,0:T(8,128)}, f32[32,512]{1,0:T(8,128)}, f32[16,128]{1,0:T(8,128)}) custom-call(bf16[1536,512]{1,0:T(8,128)(2,1)} %get-tuple-element.13.crow_ref, f32[1536,512]{1,0:T(8,128)} %get-tuple-element.14.momg_ref, bf16[1536,512]{1,0:T(8,128)(2,1)} %get-tuple-element.15.gsum_ref, ...), custom_call_target="tpu_custom_call" | custom-call | tf_op jit(solution)/shard_map/pallas_call | solution.py:514
  97.7 0.8 reshape.22
  98.5 0.6 reshape.23
  (3 shorter events, 0.0 us)

commit v3 on v2

v3 whole, which is shorter than its diff:
```python
import math

import jax
import jax.numpy as jnp
from jax import lax
from jax.experimental import pallas as pl
from jax.experimental.pallas import tpu as pltpu
from jax.sharding import PartitionSpec as P

MESH = pl.DeviceIdType.MESH

EPS = 1e-06
SCALE = 64.0
MARGIN = 0.35
MOMENT_RATE = 0.9
LEARN_RATE = 0.1

NX, NY, NZ = 2, 4, 8
TOK = 32
HALF = TOK // 2
GROUP = TOK * NX * NY * NZ
D = 512
SLOTS = 1536
ROWS = 2048
SB = 256
NSB = SLOTS // SB
OWN = SLOTS // 2
NCB = OWN // SB
LANES = 128
LOG2E = math.log2(math.e)
F32, BF16 = jnp.float32, jnp.bfloat16


class Sems:
    def __init__(self):
        self.n = 0

    def take(self, count):
        first = self.n
        self.n += count
        return first


_s = Sems()
AG1A, AG1B, AG2B = _s.take(7), _s.take(7), _s.take(7)
AGAP, AGAM = _s.take(8), _s.take(6)
LAB1, LAB2, TA1, TA2, TB1, TB2, POS1, POS2 = (_s.take(7) for _ in range(8))
CORE1, XLO, CORE2 = _s.take(3), _s.take(3), _s.take(3)
RSAP, RSAM, RSB = _s.take(8), _s.take(6), _s.take(3)
RS2A, RSBX, RSBZ = _s.take(7), _s.take(1), _s.take(7)
N_SEMS = _s.n


def wrap(value, n):
    return lax.rem(value + n, n)


def rows16(start, count):
    return pl.ds(pl.multiple_of(start, 16), count)


def lanes(start, count):
    return pl.ds(pl.multiple_of(start, LANES), count)


def fold(values):
    for shift in (64, 32, 16):
        values = values + pltpu.roll(values, shift, 1)
    return values


def row_norm(floats):
    return jnp.sqrt(jnp.sum(floats * floats, axis=-1, keepdims=True) + EPS)


def kernel(
    feat_ref, rowv_ref, lab_ref, rows_ref, cent_hbm, mom_hbm,
    fgrad_ref, loss_ref, crow_hbm, momg_hbm, gsum_hbm,
    cent_v, mom_v, feats, ids_ref, crow, cbf, cbt, momg, expo, soft,
    wide_lab, place, labs, lab1, lab1s, lab2, tot, losses, ta1, ta1s, ta2, tb1, tb1s, tb2, gacc, rtot, pos1, pos1s, pos2,
    csend, cown, crecv, xsend, xrecv, gown,
    ua, ub, sap, rap, sam, ram, sb_, rb_,
    wa, wb, wab, wbb, wbz, wbzb, r2a, rbx, rbz,
    ssem, rsem, lsem,
):
    rep, cls = lax.axis_index("rep"), lax.axis_index("cls")
    x, y, z = lax.div(cls, NY * NZ), lax.rem(lax.div(cls, NZ), NY), lax.rem(cls, NZ)
    x_lo, core = lax.div(rep, 2), lax.rem(rep, 2)

    def at(x, y, z):
        return (rep, (x * NY + y) * NZ + z)

    xy = [(k % NX, k // NX) for k in range(1, NX * NY)]

    def flip(dx):
        return x if dx == 0 else 1 - x

    def xy_to(k):
        dx, dy = xy[k]
        return flip(dx), wrap(y + dy, NY)

    def xy_from(k):
        dx, dy = xy[k]
        return flip(dx), wrap(y - dy, NY)

    def z_to(k):
        return wrap(z + k + 1, NZ)

    def z_from(k):
        return wrap(z - k - 1, NZ)

    xy_peers = [at(*xy_to(k), z) for k in range(7)]
    z_peers = [at(x, y, z_to(k)) for k in range(7)]
    y_peers = [at(x, wrap(y + k + 1, NY), z) for k in range(3)]
    x_peer = at(1 - x, y, z)
    core_peer = (x_lo * 2 + 1 - core, cls)
    xlo_peer = ((1 - x_lo) * 2 + core, cls)
    up_z, down_z = z_peers[0], z_peers[6]

    pending = []

    def push(src, dst, sem, device):
        copy = pltpu.make_async_remote_copy(
            src_ref=src, dst_ref=dst, send_sem=ssem.at[sem], recv_sem=rsem.at[sem],
            device_id=device, device_id_type=MESH,
        )
        copy.start()
        pending.append(copy)

    def arrived(dst, sem):
        pltpu.make_async_remote_copy(
            src_ref=dst, dst_ref=dst, send_sem=ssem.at[sem], recv_sem=rsem.at[sem],
            device_id=core_peer, device_id_type=MESH,
        ).wait_recv()

    stores = []

    def store(src, dst, sem):
        copy = pltpu.make_async_copy(src, dst, lsem.at[sem])
        copy.start()
        stores.append(copy)

    barrier = pltpu.get_barrier_semaphore()
    greet = xy_peers + z_peers + [core_peer, xlo_peer]
    for device in greet:
        pl.semaphore_signal(barrier, inc=1, device_id=device, device_id_type=MESH)

    load_c = pltpu.make_async_copy(cent_hbm, cent_v, lsem.at[0])
    load_m = pltpu.make_async_copy(mom_hbm, mom_v, lsem.at[1])
    load_c.start()
    load_m.start()

    half = GROUP // 2
    my_q, my_b = x * NY + y, y * NX + x

    floats = feat_ref[...].astype(F32)
    unit = (floats / row_norm(floats)).astype(BF16)
    own_a = rows16(z * 128 + my_q * HALF, HALF)
    own_b = rows16(half + my_b * 128 + z * HALF, HALF)
    feats[own_a, :] = unit[:HALF]
    feats[own_b, :] = unit[HALF:]

    lane = lax.broadcasted_iota(jnp.int32, (8, LANES), 1)
    row = lax.broadcasted_iota(jnp.int32, (8, LANES), 0)
    wide_lab[...] = jnp.zeros((8, LANES), jnp.int32)
    wide_lab[0:1, 0:TOK] = lab_ref[...]
    own_lab = jnp.broadcast_to(wide_lab[0:1, :], (8, LANES))
    lab_a = fold(jnp.where(lane < HALF, own_lab, 0))
    lab_b = fold(jnp.where((lane >= HALF) & (lane < TOK), own_lab, 0))
    place[0:8, :] = jnp.where((row == z) & (lax.div(lane, HALF) == my_q), lab_a, 0)
    place[8:16, :] = jnp.where((row == my_b) & (lax.div(lane, HALF) == z), lab_b, 0)

    pl.semaphore_wait(barrier, len(greet))

    for k in range(7):
        push(place, lab1.at[k], LAB1 + k, xy_peers[k])
    for k in range(7):
        push(feats.at[own_a, :], feats.at[own_a, :], AG1A + k, xy_peers[k])
    for k in range(7):
        push(feats.at[own_b, :], feats.at[own_b, :], AG1B + k, z_peers[k])

    for b in range(SLOTS // LANES):
        wide = jnp.broadcast_to(rowv_ref[b : b + 1, :].astype(F32), (LANES, LANES))
        ids_ref[b * LANES : (b + 1) * LANES, :] = wide.T.astype(jnp.int32) + cls * ROWS

    load_c.wait()

    def pick(sb):
        part = slice(sb * SB, (sb + 1) * SB)
        ids = ids_ref[part, :] - cls * ROWS
        col = lax.broadcasted_iota(jnp.int32, (SB, LANES), 1)
        hot = jnp.concatenate(
            [jnp.where(ids == col + j * LANES, 1.0, 0.0).astype(BF16) for j in range(ROWS // LANES)],
            axis=1,
        )
        got = jnp.dot(hot, cent_v[...], preferred_element_type=F32)
        crow[part, :] = got.astype(BF16)
        cbf[part, :] = (got * (1.0 / row_norm(got))).astype(BF16)

    for sb in range(4):
        pick(sb)

    def blk_b(px, py):
        return feats.at[rows16(half + (py * NX + px) * 128, 128), :]

    for k in range(7):
        arrived(lab1.at[k], LAB1 + k)
    lab1s[...] = place[...] + sum(lab1[k] for k in range(7))
    for k in range(7):
        push(lab1s, lab2.at[k], LAB2 + k, z_peers[k])

    for k in range(7):
        px, py = xy_from(k)
        arrived(feats.at[rows16(z * 128 + (px * NY + py) * HALF, HALF), :], AG1A + k)
    def part_of(zb, h):
        return feats.at[rows16(zb * 128 + h * 64, 64), :]

    for h in range(2):
        push(part_of(z, h), part_of(z, h), AGAP + h, up_z)
        push(part_of(z, h), part_of(z, h), AGAM + h, down_z)
    for k in range(7):
        arrived(feats.at[rows16(half + my_b * 128 + z_from(k) * HALF, HALF), :], AG1B + k)
    for k in range(7):
        push(blk_b(x, y), blk_b(x, y), AG2B + k, xy_peers[k])

    for sb in range(4, NSB):
        pick(sb)
    store(crow, crow_hbm, 2)

    def logits(tiles):
        block = jnp.concatenate([feats[rows16(t * LANES, LANES), :] for t in tiles], axis=0)
        rows = [labs[pl.ds(t, 1), :] for t in tiles]
        sums = [jnp.zeros((8, LANES), F32) for _ in range(4)]
        for sb in range(NSB):
            part = slice(sb * SB, (sb + 1) * SB)
            cosine = lax.dot_general(
                cbf[part, :], block, (((1,), (1,)), ((), ())), preferred_element_type=F32
            )
            ids = ids_ref[part, :]
            for h, t in enumerate(tiles):
                cos_h = cosine[:, h * LANES : (h + 1) * LANES]
                match = ids == rows[h]
                logit = SCALE * (cos_h - jnp.where(match, MARGIN, 0.0))
                e = jnp.exp2((logit - SCALE) * LOG2E)
                expo[part, lanes(t * LANES, LANES)] = e
                sums[h] += jnp.sum(e.reshape(SB // 8, 8, LANES), axis=0)
                hit = jnp.where(match, logit, 0.0)
                sums[2 + h] += jnp.sum(hit.reshape(SB // 8, 8, LANES), axis=0)
        for h, t in enumerate(tiles):
            tot[pl.ds(t, 1), :] = jnp.sum(sums[h], axis=0, keepdims=True)
            tot[pl.ds(16 + t, 1), :] = jnp.sum(sums[2 + h], axis=0, keepdims=True)

    def ring(s):
        zp, zm = wrap(z - 1 - s, NZ), wrap(z + 1 + s, NZ)
        for h in range(2):
            p, m = part_of(zp, h), part_of(zm, h)
            arrived(p, AGAP + 2 * s + h)
            if s < 3:
                push(p, p, AGAP + 2 * s + 2 + h, up_z)
                arrived(m, AGAM + 2 * s + h)
            if s < 2:
                push(m, m, AGAM + 2 * s + 2 + h, down_z)
        return zp, zm

    def plane(k):
        px, py = xy_from(k)
        arrived(blk_b(px, py), AG2B + k)
        return 8 + py * NX + px

    load_m.wait()

    def pick_m(j, carry):
        for u in range(16):
            i = j * 16 + u
            momg[pl.ds(i, 1), :] = mom_v[pl.ds(rows_ref[i], 1), :]
        return carry

    def pick_part(part):
        lax.fori_loop(part * SLOTS // 64, (part + 1) * SLOTS // 64, pick_m, 0)

    pick_part(0)
    near = ring(0)
    for k in range(7):
        arrived(lab2.at[k], LAB2 + k)
    labs[...] = lab1s[...] + sum(lab2[k] for k in range(7))
    logits((z, 8 + my_b))
    logits(near)
    pick_part(1)
    pick_part(2)
    near = ring(1)
    logits(near)
    pick_part(3)
    store(momg, momg_hbm, 3)
    for sb in range(NSB):
        cbt[:, sb * SB : (sb + 1) * SB] = cbf[sb * SB : (sb + 1) * SB, :].T
    near = ring(2)
    logits((plane(0), plane(1)))
    logits((plane(2), plane(3)))
    logits((plane(4), plane(5)))
    logits((plane(6), near[1]))

    def push_plane(src, dst, sem):
        for k in range(7):
            push(src, dst.at[k], sem + k, xy_peers[k])

    def push_z(src, dst, sem):
        for k in range(7):
            push(src, dst.at[k], sem + k, z_peers[k])

    def gathered(own, parts, sem):
        for k in range(7):
            arrived(parts.at[k], sem + k)
        return own + sum(parts[k] for k in range(7))

    push_plane(tot.at[8:16, :], tb1, TB1)
    far = ring(3)[0]
    logits((near[0], far))
    push_plane(tot.at[0:8, :], ta1, TA1)
    tb1s[...] = gathered(tot[8:16, :], tb1, TB1)
    push_z(tb1s, tb2, TB2)
    ta1s[...] = gathered(tot[0:8, :], ta1, TA1)
    push_z(ta1s, ta2, TA2)
    push_plane(tot.at[16:32, :], pos1, POS1)

    def soften(first, tiles):
        part = pl.ds(pl.multiple_of(first, SB), SB)
        for t in tiles:
            col = lanes(t * LANES, LANES)
            value = expo[part, col] * rtot[pl.ds(t, 1), :]
            match = jnp.where(ids_ref[part, :] == labs[pl.ds(t, 1), :], 1.0, 0.0)
            soft[part, col] = (value - match).astype(BF16)

    def feature_part(tiles):
        cols = jnp.concatenate([soft[:, lanes(t * LANES, LANES)] for t in tiles], axis=1)
        return SCALE * jnp.dot(cbt[...], cols, preferred_element_type=F32)

    def center_half_b(first):
        part = pl.ds(pl.multiple_of(first, SB), SB)
        gacc[part, :] = jnp.dot(soft[part, half:], feats[half:, :], preferred_element_type=F32)

    def center_grad(first):
        soften(first, range(8))
        part = pl.ds(pl.multiple_of(first, SB), SB)
        grad = jnp.dot(soft[part, :half], feats[:half, :], preferred_element_type=F32)
        return (SCALE * (gacc[part, :] + grad)).astype(BF16)

    mine, other = core * OWN, (1 - core) * OWN

    def grad_other(i):
        csend[i] = center_grad(other + i * SB)
        push(csend.at[i], crecv.at[i], CORE1 + i, core_peer)

    def grad_mine(i):
        cown[i] = center_grad(mine + i * SB)

    def join_cores(i):
        arrived(crecv.at[i], CORE1 + i)
        xsend[i] = (cown[i].astype(F32) + crecv[i].astype(F32)).astype(BF16)
        push(xsend.at[i], xrecv.at[i], XLO + i, xlo_peer)

    def tiles_a(s):
        return wrap(z + 4 - s, NZ), wrap(z - 3 + s, NZ)

    def tiles_b(yb):
        return 8 + yb * NX, 8 + yb * NX + 1

    def ring_sum(s):
        for h in range(2):
            part = slice(h * 256, (h + 1) * 256)
            plus = ua[s, part, :128]
            if s:
                arrived(rap.at[s - 1, part], RSAP + 2 * s - 2 + h)
                plus = plus + rap[s - 1, part].astype(F32)
            sap[s, part] = plus.astype(BF16)
            push(sap.at[s, part], rap.at[s, part], RSAP + 2 * s + h, up_z)
            if s < 3:
                minus = ua[s, part, 128:]
                if s:
                    arrived(ram.at[s - 1, part], RSAM + 2 * s - 2 + h)
                    minus = minus + ram[s - 1, part].astype(F32)
                sam[s, part] = minus.astype(BF16)
                push(sam.at[s, part], ram.at[s, part], RSAM + 2 * s + h, down_z)

    def part_a(s):
        ua[s] = feature_part(tiles_a(s))

    y_to = [wrap(y + k + 1, NY) for k in range(3)]

    def send_b(k):
        sb_[k] = feature_part(tiles_b(y_to[k])).astype(BF16)
        push(sb_.at[k], rb_.at[k], RSB + k, y_peers[k])

    totals_b = gathered(tb1s[...], tb2, TB2)
    rtot[8:16, :] = 1.0 / totals_b
    for k in (1, 0, 2):
        for sb in range(NSB):
            soften(sb * SB, tiles_b(y_to[k]))
        send_b(k)
    for sb in range(NSB):
        soften(sb * SB, tiles_b(y))
    for sb in range(NSB):
        center_half_b(sb * SB)

    totals_a = gathered(ta1s[...], ta2, TA2)
    rtot[0:8, :] = 1.0 / totals_a
    grad_other(0)
    grad_mine(0)
    for i in range(1, NCB):
        soften(other + i * SB, tiles_a(0))
        soften(mine + i * SB, tiles_a(0))
    part_a(0)
    ring_sum(0)
    grad_other(1)
    grad_mine(1)
    join_cores(0)
    grad_other(2)
    grad_mine(2)
    part_a(1)
    pos1s[...] = gathered(tot[16:32, :], pos1, POS1)
    push_z(pos1s, pos2, POS2)
    join_cores(1)
    ring_sum(1)
    join_cores(2)
    part_a(2)
    part_a(3)
    ub[...] = feature_part(tiles_b(y))
    ring_sum(2)

    positive = gathered(pos1s[...], pos2, POS2)
    losses[0:8, :] = jnp.log(totals_a) + SCALE - positive[:8]
    losses[8:16, :] = jnp.log(totals_b) + SCALE - positive[8:]
    lane = lax.broadcasted_iota(jnp.int32, (8, LANES), 1)
    loss_a = jnp.broadcast_to(losses[pl.ds(z, 1), :], (8, LANES))
    loss_b = jnp.broadcast_to(losses[pl.ds(8 + my_b, 1), :], (8, LANES))
    loss_a = fold(jnp.where(lax.div(lane, HALF) == my_q, loss_a, 0.0))
    loss_b = fold(jnp.where(lax.div(lane, HALF) == z, loss_b, 0.0))
    loss_ref[...] = jnp.where(lane < HALF, loss_a, loss_b)

    def finish_center(i):
        arrived(xrecv.at[i], XLO + i)
        gown[i] = (xsend[i].astype(F32) + xrecv[i].astype(F32)).astype(BF16)
        place_i = gsum_hbm.at[rows16(mine + i * SB, SB), :]
        push(gown.at[i], place_i, CORE2 + i, core_peer)
        store(gown.at[i], place_i, 4 + i)

    finish_center(0)
    ring_sum(3)

    for k in range(3):
        arrived(rb_.at[k], RSB + k)
    slab = ub[...] + sum(rb_[k].astype(F32) for k in range(3))
    for h in range(2):
        turned = slab[:, h * 128 : (h + 1) * 128].T
        for q in range(NZ):
            wb[q * TOK + h * HALF : q * TOK + (h + 1) * HALF, :] = turned[q * HALF : (q + 1) * HALF, :]
    wbb[...] = wb[...].astype(BF16)
    for k in range(7):
        push(wbb.at[rows16(z_to(k) * TOK, TOK), :], rbz.at[k], RSBZ + k, z_peers[k])

    finish_center(1)

    for h in range(2):
        part = slice(h * 256, (h + 1) * 256)
        arrived(ram.at[2, part], RSAM + 4 + h)
        arrived(rap.at[3, part], RSAP + 6 + h)
    slab = ua[3][:, 128:] + rap[3].astype(F32) + ram[2].astype(F32)
    wa[...] = slab.T
    wab[...] = wa[...].astype(BF16)
    for k in range(7):
        px, py = xy_to(k)
        push(wab.at[rows16((px * NY + py) * HALF, HALF), :], r2a.at[k], RS2A + k, xy_peers[k])

    for k in range(7):
        arrived(rbz.at[k], RSBZ + k)
    wbz[...] = wb[rows16(z * TOK, TOK), :] + sum(rbz[k].astype(F32) for k in range(7))
    wbzb[...] = wbz[rows16((1 - x) * HALF, HALF), :].astype(BF16)
    push(wbzb, rbx, RSBX, x_peer)

    finish_center(2)

    for k in range(7):
        arrived(r2a.at[k], RS2A + k)
    g_a = wa[rows16(my_q * HALF, HALF), :] + sum(r2a[k].astype(F32) for k in range(7))
    arrived(rbx, RSBX)
    g_b = wbz[rows16(x * HALF, HALF), :] + rbx[...].astype(F32)
    for h, grad in enumerate((g_a, g_b)):
        own = feat_ref[h * HALF : (h + 1) * HALF, :].astype(F32)
        norm = row_norm(own)
        unit_f = own / norm
        dot = jnp.sum(unit_f * grad, axis=1, keepdims=True)
        fgrad_ref[h * HALF : (h + 1) * HALF, :] = (grad - unit_f * dot) / norm

    for i in range(NCB):
        arrived(gsum_hbm.at[rows16(other + i * SB, SB), :], CORE2 + i)
    for copy in pending:
        copy.wait_send()
    for copy in stores:
        copy.wait()


def update(
    crow_hbm, momg_hbm, gsum_hbm, fgrad_hbm, loss_ref, newc_hbm, newm_hbm, fout_hbm, lout_ref,
    rows_v, mom_v, grad_v, newc_v, newm_v, sem,
):
    n = SLOTS // SB
    pass_on = pltpu.make_async_copy(fgrad_hbm, fout_hbm, sem.at[5 * n])
    pass_on.start()

    def part(i):
        return pl.ds(i * SB, SB)

    loads, stores = [], []
    for i in range(n):
        for j, (src, dst) in enumerate(((crow_hbm, rows_v), (gsum_hbm, grad_v), (momg_hbm, mom_v))):
            copy = pltpu.make_async_copy(src.at[part(i), :], dst.at[part(i), :], sem.at[j * n + i])
            copy.start()
            loads.append(copy)
    lout_ref[...] = loss_ref[0:1, 0:TOK]
    for i in range(n):
        for copy in loads[3 * i : 3 * i + 3]:
            copy.wait()
        rows, grad = rows_v[part(i), :].astype(F32), grad_v[part(i), :].astype(F32)
        inverse = 1.0 / row_norm(rows)
        along = jnp.sum(rows * grad, axis=1, keepdims=True) * (inverse * inverse * inverse)
        new_m = MOMENT_RATE * mom_v[part(i), :] + (grad * inverse - rows * along)
        newm_v[part(i), :] = new_m
        newc_v[part(i), :] = (rows - LEARN_RATE * new_m).astype(BF16)
        for j, (src, dst) in enumerate(((newm_v, newm_hbm), (newc_v, newc_hbm))):
            copy = pltpu.make_async_copy(src.at[part(i), :], dst.at[part(i), :], sem.at[(3 + j) * n + i])
            copy.start()
            stores.append(copy)
    for copy in stores:
        copy.wait()
    pass_on.wait()


def local(features, centers, momentum, sample_rows, labels):
    vm = pl.BlockSpec(memory_space=pltpu.VMEM)
    hbm = pl.BlockSpec(memory_space=pl.ANY)
    v = pltpu.VMEM
    sds = jax.ShapeDtypeStruct
    f_grad, loss, crow, momg, gsum = pl.pallas_call(
        kernel,
        out_shape=(
            sds((TOK, D), F32),
            sds((8, LANES), F32),
            sds((SLOTS, D), BF16),
            sds((SLOTS, D), F32),
            sds((SLOTS, D), BF16),
        ),
        in_specs=[vm, vm, vm, pl.BlockSpec(memory_space=pltpu.SMEM), hbm, hbm],
        out_specs=(vm, vm, hbm, hbm, hbm),
        scratch_shapes=[
            v((ROWS, D), BF16), v((ROWS, D), F32), v((GROUP, D), BF16), v((SLOTS, LANES), jnp.int32),
            v((SLOTS, D), BF16), v((SLOTS, D), BF16), v((D, SLOTS), BF16), v((SLOTS, D), F32),
            v((SLOTS, GROUP), F32), v((SLOTS, GROUP), BF16),
            v((8, LANES), jnp.int32), v((16, LANES), jnp.int32), v((16, LANES), jnp.int32),
            v((7, 16, LANES), jnp.int32),
            v((16, LANES), jnp.int32), v((7, 16, LANES), jnp.int32),
            v((32, LANES), F32), v((16, LANES), F32),
            v((7, 8, LANES), F32), v((8, LANES), F32), v((7, 8, LANES), F32),
            v((7, 8, LANES), F32), v((8, LANES), F32), v((7, 8, LANES), F32), v((SLOTS, D), F32),
            v((16, LANES), F32), v((7, 16, LANES), F32), v((16, LANES), F32), v((7, 16, LANES), F32),
            v((NCB, SB, D), BF16), v((NCB, SB, D), BF16), v((NCB, SB, D), BF16),
            v((NCB, SB, D), BF16), v((NCB, SB, D), BF16), v((NCB, SB, D), BF16),
            v((4, D, 256), F32), v((D, 256), F32),
            v((4, D, 128), BF16), v((4, D, 128), BF16), v((3, D, 128), BF16), v((3, D, 128), BF16),
            v((3, D, 256), BF16), v((3, D, 256), BF16),
            v((128, D), F32), v((256, D), F32), v((128, D), BF16), v((256, D), BF16),
            v((TOK, D), F32), v((HALF, D), BF16),
            v((7, HALF, D), BF16), v((HALF, D), BF16), v((7, TOK, D), BF16),
            pltpu.SemaphoreType.DMA((N_SEMS,)), pltpu.SemaphoreType.DMA((N_SEMS,)),
            pltpu.SemaphoreType.DMA((4 + NCB,)),
        ],
        compiler_params=pltpu.CompilerParams(
            collective_id=0, has_side_effects=True, vmem_limit_bytes=60 * 1024 * 1024
        ),
    )(
        features,
        sample_rows.reshape(SLOTS // LANES, LANES),
        labels.reshape(1, TOK),
        sample_rows,
        centers,
        momentum,
    )
    new_c, new_m, f_grad, loss = pl.pallas_call(
        update,
        out_shape=(
            sds((SLOTS, D), BF16), sds((SLOTS, D), F32), sds((TOK, D), F32), sds((1, TOK), F32),
        ),
        in_specs=[hbm, hbm, hbm, hbm, vm],
        out_specs=(hbm, hbm, hbm, vm),
        scratch_shapes=[
            v((SLOTS, D), BF16), v((SLOTS, D), F32), v((SLOTS, D), BF16),
            v((SLOTS, D), BF16), v((SLOTS, D), F32),
            pltpu.SemaphoreType.DMA((5 * NSB + 1,)),
        ],
        compiler_params=pltpu.CompilerParams(vmem_limit_bytes=60 * 1024 * 1024),
    )(crow, momg, gsum, f_grad, loss)
    return (f_grad, loss.reshape(TOK), new_c, new_m)


def solution(mesh):
    in_specs = (
        P(("rep", "cls"), None),
        P("cls", None),
        P("cls", None),
        P("cls"),
        P(("rep", "cls")),
    )
    out_specs = (P(("rep", "cls"), None), P(("rep", "cls")), P("cls", None), P("cls", None))
    return jax.shard_map(local, mesh=mesh, in_specs=in_specs, out_specs=out_specs, check_vma=False)
```

time: 99.5 us -> 88.1 us (0.89)
  Pallas kernels: 95.6 us -> 86.7 us
  local copies, waits for them, and re-layouts: 2.76 us -> 0 us
    pallas_call x2, Pallas kernels: 95.6 us -> 86.7 us  [the longest x1 80.4 us: local(): pl.pallas_call(kernel, out_shape=(sds((TOK, D), F32), sds((8, LANES), F32...]
    another operation x3 -> x0, local copies, waits for them, and re-layouts: 1.39 us -> none  [local(): jnp.tile(labels.reshape(2, HALF), (1, LANES // HALF))]
    reshape x2 -> x0, local copies, waits for them, and re-layouts: 1.36 us -> none  [the longest x1 0.77 us: local(): flat = loss.reshape(GROUP // HALF, HALF)]
where the time goes in v3:
time: 88.1 us; the launch traced here: 87.6 us
  Pallas kernels  86.7 us (98%)
    pallas_call x1, Pallas kernels, local(): pl.pallas_call(kernel, out_shape=(sds((TOK, D), F32), sds((8, LANES), F32...  80.4 us
    pallas_call x1, Pallas kernels, local(): pl.pallas_call(update, out_shape=(sds((SLOTS, D), BF16), sds((SLOTS, D),...  6.33 us

profile of v3, /device:TPU:2, one launch (start us, length us, event | category | flops | bytes accessed | tf_op | source)
XLA Modules:
  0.0 87.6 jit_solution(4893913227799204601)
XLA Ops:
  0.6 80.4 %shard_map.84 = (f32[32,512]{1,0:T(8,128)}, f32[8,128]{1,0:T(8,128)}, bf16[1536,512]{1,0:T(8,128)(2,1)}, f32[1536,512]{1,0:T(8,128)}, bf16[1536,512]{1,0:T(8,128)(2,1)}) custom-call(bf16[32,512]{1,0:T(8,128)(2,1)} %feat_ref.1, s32[12,128]{1,0:T(8,128)} %bitcast.3, s32[1,32]{1,0:T(1,128)} %bitcast.4, s32[1536]{0:T(1024)} %rows_ref.1, ...), custom_call_target="tpu_custom_call" | custom-call | tf_op jit(solution)/shard_map/pallas_call | solution.py:542
  81.1 6.3 %shard_map.85 = (bf16[1536,512]{1,0:T(8,128)(2,1)}, f32[1536,512]{1,0:T(8,128)}, f32[32,512]{1,0:T(8,128)}, f32[1,32]{1,0:T(1,128)}) custom-call(bf16[1536,512]{1,0:T(8,128)(2,1)} %get-tuple-element.13.crow_hbm, f32[1536,512]{1,0:T(8,128)} %get-tuple-element.14.momg_hbm, bf16[1536,512]{1,0:T(8,128)(2,1)} %get-tuple-element.15.gsum_hbm, ...), custom_call_target="tpu_custom_call" | custom-call | tf_op jit(solution)/shard_map/pallas_call | solution.py:586

commit v4 on v3

--- a/solution.py
+++ b/solution.py
@@ -26,6 +26,7 @@
 NSB = SLOTS // SB
 OWN = SLOTS // 2
 NCB = OWN // SB
+UB = 512
 LANES = 128
 LOG2E = math.log2(math.e)
 F32, BF16 = jnp.float32, jnp.bfloat16
@@ -44,7 +45,7 @@
 _s = Sems()
 AG1A, AG1B, AG2B = _s.take(7), _s.take(7), _s.take(7)
 AGAP, AGAM = _s.take(8), _s.take(6)
-LAB1, LAB2, TA1, TA2, TB1, TB2, POS1, POS2 = (_s.take(7) for _ in range(8))
+LAB1, LAB2, TOT1, TOT2, POS1, POS2 = (_s.take(7) for _ in range(6))
 CORE1, XLO, CORE2 = _s.take(3), _s.take(3), _s.take(3)
 RSAP, RSAM, RSB = _s.take(8), _s.take(6), _s.take(3)
 RS2A, RSBX, RSBZ = _s.take(7), _s.take(1), _s.take(7)
@@ -77,9 +78,9 @@
     feat_ref, rowv_ref, lab_ref, rows_ref, cent_hbm, mom_hbm,
     fgrad_ref, loss_ref, crow_hbm, momg_hbm, gsum_hbm,
     cent_v, mom_v, feats, ids_ref, crow, cbf, cbt, momg, expo, soft,
-    wide_lab, place, labs, lab1, lab1s, lab2, tot, losses, ta1, ta1s, ta2, tb1, tb1s, tb2, gacc, rtot, pos1, pos1s, pos2,
+    wide_lab, place, labs, lab1, lab1s, lab2, tot, losses, tot1, tot1s, tot2, rtot, pm1, pos1, pos1s, pos2,
     csend, cown, crecv, xsend, xrecv, gown,
-    ua, ub, sap, rap, sam, ram, sb_, rb_,
+    up, mm, sap, rap, sam, ram, sb_, rb_,
     wa, wb, wab, wbb, wbz, wbzb, r2a, rbx, rbz,
     ssem, rsem, lsem,
 ):
@@ -243,6 +244,7 @@
                 logit = SCALE * (cos_h - jnp.where(match, MARGIN, 0.0))
                 e = jnp.exp2((logit - SCALE) * LOG2E)
                 expo[part, lanes(t * LANES, LANES)] = e
+                soft[part, lanes(t * LANES, LANES)] = jnp.where(match, 0.0, e).astype(BF16)
                 sums[h] += jnp.sum(e.reshape(SB // 8, 8, LANES), axis=0)
                 hit = jnp.where(match, logit, 0.0)
                 sums[2 + h] += jnp.sum(hit.reshape(SB // 8, 8, LANES), axis=0)
@@ -312,15 +314,32 @@
             arrived(parts.at[k], sem + k)
         return own + sum(parts[k] for k in range(7))
 
-    push_plane(tot.at[8:16, :], tb1, TB1)
     far = ring(3)[0]
     logits((near[0], far))
-    push_plane(tot.at[0:8, :], ta1, TA1)
-    tb1s[...] = gathered(tot[8:16, :], tb1, TB1)
-    push_z(tb1s, tb2, TB2)
-    ta1s[...] = gathered(tot[0:8, :], ta1, TA1)
-    push_z(ta1s, ta2, TA2)
+    push_plane(tot.at[0:16, :], tot1, TOT1)
+
+    def other_classes(k):
+        col = slice(k * 256, (k + 1) * 256)
+        up[:, col] = jnp.dot(cbt[...], soft[:, col], preferred_element_type=F32)
+
+    def label_center(k):
+        col = slice(k * 256, (k + 1) * 256)
+        rows = [labs[2 * k + h : 2 * k + h + 1, :] for h in range(2)]
+        match = jnp.concatenate(
+            [jnp.where(ids_ref[...] == r, 1.0, 0.0).astype(BF16) for r in rows], axis=1
+        )
+        mm[:, col] = jnp.dot(cbt[...], match, preferred_element_type=F32).astype(BF16)
+
+    for k in range(8):
+        other_classes(k)
+    tot1s[...] = gathered(tot[0:16, :], tot1, TOT1)
+    push_z(tot1s, tot2, TOT2)
     push_plane(tot.at[16:32, :], pos1, POS1)
+    for k in range(8):
+        label_center(k)
+    totals = gathered(tot1s[...], tot2, TOT2)
+    rtot[...] = 1.0 / totals
+    pm1[...] = jnp.exp2((tot[16:32, :] - SCALE) * LOG2E) * rtot[...] - 1.0
 
     def soften(first, tiles):
         part = pl.ds(pl.multiple_of(first, SB), SB)
@@ -330,19 +349,14 @@
             match = jnp.where(ids_ref[part, :] == labs[pl.ds(t, 1), :], 1.0, 0.0)
             soft[part, col] = (value - match).astype(BF16)
 
-    def feature_part(tiles):
-        cols = jnp.concatenate([soft[:, lanes(t * LANES, LANES)] for t in tiles], axis=1)
-        return SCALE * jnp.dot(cbt[...], cols, preferred_element_type=F32)
-
-    def center_half_b(first):
+    def feature_part(t):
+        col, row = lanes(t * LANES, LANES), pl.ds(t, 1)
+        return SCALE * (up[:, col] * rtot[row, :] + mm[:, col].astype(F32) * pm1[row, :])
+
+    def center_grad(first):
+        soften(first, range(GROUP // LANES))
         part = pl.ds(pl.multiple_of(first, SB), SB)
-        gacc[part, :] = jnp.dot(soft[part, half:], feats[half:, :], preferred_element_type=F32)
-
-    def center_grad(first):
-        soften(first, range(8))
-        part = pl.ds(pl.multiple_of(first, SB), SB)
-        grad = jnp.dot(soft[part, :half], feats[:half, :], preferred_element_type=F32)
-        return (SCALE * (gacc[part, :] + grad)).astype(BF16)
+        return (SCALE * jnp.dot(soft[part, :], feats[...], preferred_element_type=F32)).astype(BF16)
 
     mine, other = core * OWN, (1 - core) * OWN
 
@@ -365,70 +379,51 @@
         return 8 + yb * NX, 8 + yb * NX + 1
 
     def ring_sum(s):
+        tp, tm = tiles_a(s)
+        plus_all, minus_all = feature_part(tp), feature_part(tm) if s < 3 else None
         for h in range(2):
             part = slice(h * 256, (h + 1) * 256)
-            plus = ua[s, part, :128]
+            plus = plus_all[part]
             if s:
                 arrived(rap.at[s - 1, part], RSAP + 2 * s - 2 + h)
                 plus = plus + rap[s - 1, part].astype(F32)
             sap[s, part] = plus.astype(BF16)
             push(sap.at[s, part], rap.at[s, part], RSAP + 2 * s + h, up_z)
             if s < 3:
-                minus = ua[s, part, 128:]
+                minus = minus_all[part]
                 if s:
                     arrived(ram.at[s - 1, part], RSAM + 2 * s - 2 + h)
                     minus = minus + ram[s - 1, part].astype(F32)
                 sam[s, part] = minus.astype(BF16)
                 push(sam.at[s, part], ram.at[s, part], RSAM + 2 * s + h, down_z)
 
-    def part_a(s):
-        ua[s] = feature_part(tiles_a(s))
-
     y_to = [wrap(y + k + 1, NY) for k in range(3)]
 
     def send_b(k):
-        sb_[k] = feature_part(tiles_b(y_to[k])).astype(BF16)
+        for h, t in enumerate(tiles_b(y_to[k])):
+            sb_[k, :, h * LANES : (h + 1) * LANES] = feature_part(t).astype(BF16)
         push(sb_.at[k], rb_.at[k], RSB + k, y_peers[k])
 
-    totals_b = gathered(tb1s[...], tb2, TB2)
-    rtot[8:16, :] = 1.0 / totals_b
-    for k in (1, 0, 2):
-        for sb in range(NSB):
-            soften(sb * SB, tiles_b(y_to[k]))
-        send_b(k)
-    for sb in range(NSB):
-        soften(sb * SB, tiles_b(y))
-    for sb in range(NSB):
-        center_half_b(sb * SB)
-
-    totals_a = gathered(ta1s[...], ta2, TA2)
-    rtot[0:8, :] = 1.0 / totals_a
+    ring_sum(0)
+    send_b(1)
+    send_b(0)
+    send_b(2)
     grad_other(0)
     grad_mine(0)
-    for i in range(1, NCB):
-        soften(other + i * SB, tiles_a(0))
-        soften(mine + i * SB, tiles_a(0))
-    part_a(0)
-    ring_sum(0)
     grad_other(1)
+    join_cores(0)
+    ring_sum(1)
     grad_mine(1)
-    join_cores(0)
     grad_other(2)
-    grad_mine(2)
-    part_a(1)
+    join_cores(1)
     pos1s[...] = gathered(tot[16:32, :], pos1, POS1)
     push_z(pos1s, pos2, POS2)
-    join_cores(1)
-    ring_sum(1)
+    grad_mine(2)
+    ring_sum(2)
     join_cores(2)
-    part_a(2)
-    part_a(3)
-    ub[...] = feature_part(tiles_b(y))
-    ring_sum(2)
 
     positive = gathered(pos1s[...], pos2, POS2)
-    losses[0:8, :] = jnp.log(totals_a) + SCALE - positive[:8]
-    losses[8:16, :] = jnp.log(totals_b) + SCALE - positive[8:]
+    losses[...] = jnp.log(totals) + SCALE - positive
     lane = lax.broadcasted_iota(jnp.int32, (8, LANES), 1)
     loss_a = jnp.broadcast_to(losses[pl.ds(z, 1), :], (8, LANES))
     loss_b = jnp.broadcast_to(losses[pl.ds(8 + my_b, 1), :], (8, LANES))
@@ -448,9 +443,9 @@
 
     for k in range(3):
         arrived(rb_.at[k], RSB + k)
-    slab = ub[...] + sum(rb_[k].astype(F32) for k in range(3))
-    for h in range(2):
-        turned = slab[:, h * 128 : (h + 1) * 128].T
+    for h, t in enumerate(tiles_b(y)):
+        slab = feature_part(t) + sum(rb_[k, :, h * LANES : (h + 1) * LANES].astype(F32) for k in range(3))
+        turned = slab.T
         for q in range(NZ):
             wb[q * TOK + h * HALF : q * TOK + (h + 1) * HALF, :] = turned[q * HALF : (q + 1) * HALF, :]
     wbb[...] = wb[...].astype(BF16)
@@ -463,7 +458,7 @@
         part = slice(h * 256, (h + 1) * 256)
         arrived(ram.at[2, part], RSAM + 4 + h)
         arrived(rap.at[3, part], RSAP + 6 + h)
-    slab = ua[3][:, 128:] + rap[3].astype(F32) + ram[2].astype(F32)
+    slab = feature_part(z) + rap[3].astype(F32) + ram[2].astype(F32)
     wa[...] = slab.T
     wab[...] = wa[...].astype(BF16)
     for k in range(7):
@@ -502,12 +497,12 @@
     crow_hbm, momg_hbm, gsum_hbm, fgrad_hbm, loss_ref, newc_hbm, newm_hbm, fout_hbm, lout_ref,
     rows_v, mom_v, grad_v, newc_v, newm_v, sem,
 ):
-    n = SLOTS // SB
+    n = SLOTS // UB
     pass_on = pltpu.make_async_copy(fgrad_hbm, fout_hbm, sem.at[5 * n])
     pass_on.start()
 
     def part(i):
-        return pl.ds(i * SB, SB)
+        return pl.ds(i * UB, UB)
 
     loads, stores = [], []
     for i in range(n):
@@ -558,12 +553,11 @@
             v((7, 16, LANES), jnp.int32),
             v((16, LANES), jnp.int32), v((7, 16, LANES), jnp.int32),
             v((32, LANES), F32), v((16, LANES), F32),
-            v((7, 8, LANES), F32), v((8, LANES), F32), v((7, 8, LANES), F32),
-            v((7, 8, LANES), F32), v((8, LANES), F32), v((7, 8, LANES), F32), v((SLOTS, D), F32),
+            v((7, 16, LANES), F32), v((16, LANES), F32), v((7, 16, LANES), F32), v((16, LANES), F32),
             v((16, LANES), F32), v((7, 16, LANES), F32), v((16, LANES), F32), v((7, 16, LANES), F32),
             v((NCB, SB, D), BF16), v((NCB, SB, D), BF16), v((NCB, SB, D), BF16),
             v((NCB, SB, D), BF16), v((NCB, SB, D), BF16), v((NCB, SB, D), BF16),
-            v((4, D, 256), F32), v((D, 256), F32),
+            v((D, GROUP), F32), v((D, GROUP), BF16),
             v((4, D, 128), BF16), v((4, D, 128), BF16), v((3, D, 128), BF16), v((3, D, 128), BF16),
             v((3, D, 256), BF16), v((3, D, 256), BF16),
             v((128, D), F32), v((256, D), F32), v((128, D), BF16), v((256, D), BF16),
@@ -593,7 +587,7 @@
         scratch_shapes=[
             v((SLOTS, D), BF16), v((SLOTS, D), F32), v((SLOTS, D), BF16),
             v((SLOTS, D), BF16), v((SLOTS, D), F32),
-            pltpu.SemaphoreType.DMA((5 * NSB + 1,)),
+            pltpu.SemaphoreType.DMA((5 * (SLOTS // UB) + 1,)),
         ],
         compiler_params=pltpu.CompilerParams(vmem_limit_bytes=60 * 1024 * 1024),
     )(crow, momg, gsum, f_grad, loss)

time: 88.1 us -> 83.8 us (0.951)
  Pallas kernels: 86.7 us -> 82.8 us
    pallas_call x1, Pallas kernels: 80.4 us -> 76.9 us  [local(): pl.pallas_call(kernel, out_shape=(sds((TOK, D), F32), sds((8, LANES), F32...]
where the time goes in v4:
time: 83.8 us; the launch traced here: 83.6 us
  Pallas kernels  82.8 us (99%)
    pallas_call x1, Pallas kernels, local(): pl.pallas_call(kernel, out_shape=(sds((TOK, D), F32), sds((8, LANES), F32...  76.9 us
    pallas_call x1, Pallas kernels, local(): pl.pallas_call(update, out_shape=(sds((SLOTS, D), BF16), sds((SLOTS, D),...  5.87 us

profile of v4, /device:TPU:2, one launch (start us, length us, event | category | flops | bytes accessed | tf_op | source)
XLA Modules:
  0.0 83.6 jit_solution(2791510872167798682)
XLA Ops:
  0.6 76.9 %shard_map.84 = (f32[32,512]{1,0:T(8,128)}, f32[8,128]{1,0:T(8,128)}, bf16[1536,512]{1,0:T(8,128)(2,1)}, f32[1536,512]{1,0:T(8,128)}, bf16[1536,512]{1,0:T(8,128)(2,1)}) custom-call(bf16[32,512]{1,0:T(8,128)(2,1)} %feat_ref.1, s32[12,128]{1,0:T(8,128)} %bitcast.3, s32[1,32]{1,0:T(1,128)} %bitcast.4, s32[1536]{0:T(1024)} %rows_ref.1, ...), custom_call_target="tpu_custom_call" | custom-call | tf_op jit(solution)/shard_map/pallas_call | solution.py:537
  77.5 5.9 %shard_map.85 = (bf16[1536,512]{1,0:T(8,128)(2,1)}, f32[1536,512]{1,0:T(8,128)}, f32[32,512]{1,0:T(8,128)}, f32[1,32]{1,0:T(1,128)}) custom-call(bf16[1536,512]{1,0:T(8,128)(2,1)} %get-tuple-element.13.crow_hbm, f32[1536,512]{1,0:T(8,128)} %get-tuple-element.14.momg_hbm, bf16[1536,512]{1,0:T(8,128)(2,1)} %get-tuple-element.15.gsum_hbm, ...), custom_call_target="tpu_custom_call" | custom-call | tf_op jit(solution)/shard_map/pallas_call | solution.py:580

commit v5 on v4

--- a/solution.py
+++ b/solution.py
@@ -227,6 +227,8 @@
     for sb in range(4, NSB):
         pick(sb)
     store(crow, crow_hbm, 2)
+    for sb in range(NSB):
+        cbt[:, sb * SB : (sb + 1) * SB] = cbf[sb * SB : (sb + 1) * SB, :].T
 
     def logits(tiles):
         block = jnp.concatenate([feats[rows16(t * LANES, LANES), :] for t in tiles], axis=0)
@@ -269,59 +271,6 @@
         arrived(blk_b(px, py), AG2B + k)
         return 8 + py * NX + px
 
-    load_m.wait()
-
-    def pick_m(j, carry):
-        for u in range(16):
-            i = j * 16 + u
-            momg[pl.ds(i, 1), :] = mom_v[pl.ds(rows_ref[i], 1), :]
-        return carry
-
-    def pick_part(part):
-        lax.fori_loop(part * SLOTS // 64, (part + 1) * SLOTS // 64, pick_m, 0)
-
-    pick_part(0)
-    near = ring(0)
-    for k in range(7):
-        arrived(lab2.at[k], LAB2 + k)
-    labs[...] = lab1s[...] + sum(lab2[k] for k in range(7))
-    logits((z, 8 + my_b))
-    logits(near)
-    pick_part(1)
-    pick_part(2)
-    near = ring(1)
-    logits(near)
-    pick_part(3)
-    store(momg, momg_hbm, 3)
-    for sb in range(NSB):
-        cbt[:, sb * SB : (sb + 1) * SB] = cbf[sb * SB : (sb + 1) * SB, :].T
-    near = ring(2)
-    logits((plane(0), plane(1)))
-    logits((plane(2), plane(3)))
-    logits((plane(4), plane(5)))
-    logits((plane(6), near[1]))
-
-    def push_plane(src, dst, sem):
-        for k in range(7):
-            push(src, dst.at[k], sem + k, xy_peers[k])
-
-    def push_z(src, dst, sem):
-        for k in range(7):
-            push(src, dst.at[k], sem + k, z_peers[k])
-
-    def gathered(own, parts, sem):
-        for k in range(7):
-            arrived(parts.at[k], sem + k)
-        return own + sum(parts[k] for k in range(7))
-
-    far = ring(3)[0]
-    logits((near[0], far))
-    push_plane(tot.at[0:16, :], tot1, TOT1)
-
-    def other_classes(k):
-        col = slice(k * 256, (k + 1) * 256)
-        up[:, col] = jnp.dot(cbt[...], soft[:, col], preferred_element_type=F32)
-
     def label_center(k):
         col = slice(k * 256, (k + 1) * 256)
         rows = [labs[2 * k + h : 2 * k + h + 1, :] for h in range(2)]
@@ -330,12 +279,52 @@
         )
         mm[:, col] = jnp.dot(cbt[...], match, preferred_element_type=F32).astype(BF16)
 
+    near = ring(0)
+    for k in range(7):
+        arrived(lab2.at[k], LAB2 + k)
+    labs[...] = lab1s[...] + sum(lab2[k] for k in range(7))
+    logits((z, 8 + my_b))
+    logits(near)
+    label_center(0)
+    label_center(1)
+    near = ring(1)
+    logits(near)
+    label_center(2)
+    label_center(3)
+    label_center(4)
+    near = ring(2)
+    logits((plane(0), plane(1)))
+    logits((plane(2), plane(3)))
+    logits((plane(4), plane(5)))
+    logits((plane(6), near[1]))
+
+    def push_plane(src, dst, sem):
+        for k in range(7):
+            push(src, dst.at[k], sem + k, xy_peers[k])
+
+    def push_z(src, dst, sem):
+        for k in range(7):
+            push(src, dst.at[k], sem + k, z_peers[k])
+
+    def gathered(own, parts, sem):
+        for k in range(7):
+            arrived(parts.at[k], sem + k)
+        return own + sum(parts[k] for k in range(7))
+
+    far = ring(3)[0]
+    logits((near[0], far))
+    push_plane(tot.at[0:16, :], tot1, TOT1)
+
+    def other_classes(k):
+        col = slice(k * 256, (k + 1) * 256)
+        up[:, col] = jnp.dot(cbt[...], soft[:, col], preferred_element_type=F32)
+
     for k in range(8):
         other_classes(k)
     tot1s[...] = gathered(tot[0:16, :], tot1, TOT1)
     push_z(tot1s, tot2, TOT2)
     push_plane(tot.at[16:32, :], pos1, POS1)
-    for k in range(8):
+    for k in range(5, 8):
         label_center(k)
     totals = gathered(tot1s[...], tot2, TOT2)
     rtot[...] = 1.0 / totals
@@ -404,6 +393,17 @@
             sb_[k, :, h * LANES : (h + 1) * LANES] = feature_part(t).astype(BF16)
         push(sb_.at[k], rb_.at[k], RSB + k, y_peers[k])
 
+    load_m.wait()
+
+    def pick_m(j, carry):
+        for u in range(16):
+            i = j * 16 + u
+            momg[pl.ds(i, 1), :] = mom_v[pl.ds(rows_ref[i], 1), :]
+        return carry
+
+    def pick_part(part):
+        lax.fori_loop(part * SLOTS // 64, (part + 1) * SLOTS // 64, pick_m, 0)
+
     ring_sum(0)
     send_b(1)
     send_b(0)
@@ -421,6 +421,8 @@
     grad_mine(2)
     ring_sum(2)
     join_cores(2)
+    pick_part(0)
+    pick_part(1)
 
     positive = gathered(pos1s[...], pos2, POS2)
     losses[...] = jnp.log(totals) + SCALE - positive
@@ -440,6 +442,7 @@
 
     finish_center(0)
     ring_sum(3)
+    pick_part(2)
 
     for k in range(3):
         arrived(rb_.at[k], RSB + k)
@@ -452,6 +455,8 @@
     for k in range(7):
         push(wbb.at[rows16(z_to(k) * TOK, TOK), :], rbz.at[k], RSBZ + k, z_peers[k])
 
+    pick_part(3)
+    store(momg, momg_hbm, 3)
     finish_center(1)
 
     for h in range(2):

time: 83.8 us -> 83.5 us (level); the launches traced: 83.6 us -> 82.3 us
  Pallas kernels: 82.8 us -> 81.5 us
    pallas_call x1, Pallas kernels: 76.9 us -> 75.6 us  [local(): pl.pallas_call(kernel, out_shape=(sds((TOK, D), F32), sds((8, LANES), F32...]
where the time goes in v5:
time: 83.5 us; the launch traced here: 82.3 us
  Pallas kernels  81.5 us (98%)
    pallas_call x1, Pallas kernels, local(): pl.pallas_call(kernel, out_shape=(sds((TOK, D), F32), sds((8, LANES), F32...  75.6 us
    pallas_call x1, Pallas kernels, local(): pl.pallas_call(update, out_shape=(sds((SLOTS, D), BF16), sds((SLOTS, D),...  5.87 us

profile of v5, /device:TPU:2, one launch (start us, length us, event | category | flops | bytes accessed | tf_op | source)
XLA Modules:
  0.0 82.3 jit_solution(12492995590986959495)
XLA Ops:
  0.6 75.6 %shard_map.84 = (f32[32,512]{1,0:T(8,128)}, f32[8,128]{1,0:T(8,128)}, bf16[1536,512]{1,0:T(8,128)(2,1)}, f32[1536,512]{1,0:T(8,128)}, bf16[1536,512]{1,0:T(8,128)(2,1)}) custom-call(bf16[32,512]{1,0:T(8,128)(2,1)} %feat_ref.1, s32[12,128]{1,0:T(8,128)} %bitcast.3, s32[1,32]{1,0:T(1,128)} %bitcast.4, s32[1536]{0:T(1024)} %rows_ref.1, ...), custom_call_target="tpu_custom_call" | custom-call | tf_op jit(solution)/shard_map/pallas_call | solution.py:542
  76.2 5.9 %shard_map.85 = (bf16[1536,512]{1,0:T(8,128)(2,1)}, f32[1536,512]{1,0:T(8,128)}, f32[32,512]{1,0:T(8,128)}, f32[1,32]{1,0:T(1,128)}) custom-call(bf16[1536,512]{1,0:T(8,128)(2,1)} %get-tuple-element.13.crow_hbm, f32[1536,512]{1,0:T(8,128)} %get-tuple-element.14.momg_hbm, bf16[1536,512]{1,0:T(8,128)(2,1)} %get-tuple-element.15.gsum_hbm, ...), custom_call_target="tpu_custom_call" | custom-call | tf_op jit(solution)/shard_map/pallas_call | solution.py:585
